TPU v7x, 128 devices: a whole 4x4x4 slice. The times are simulated.
128 devices in a mesh: net: 32 (over x, y, core), dev: 4 (over z).
Axes of the slice: x: 4, y: 4, z: 4, core: 2. Of those that a mesh axis runs over, the one named last changes fastest.
Arguments:
- zinv: float32 [128, 1024, 1024], P('net', 'dev')
- source: float32 [131072], P('net'), may hold values from -4 to 4
- model_state: float32 [16384, 128], P(('net', 'dev')), may hold values from -6 to 6
- propagator: float32 [16384, 128, 128], P(('net', 'dev')), may hold values from -0.4375 to 0.4375
- input_gain: float32 [16384, 128], P(('net', 'dev')), may hold values from -3 to 3
- output_gain: float32 [16384, 128], P(('net', 'dev')), may hold values from -0.5 to 0.5
- model_owner: int32 [16384, 1], P(('net', 'dev')), may hold values from 0 to 31; in each aligned block of 128 rows (0 to 127, 128 to 255, ...) at most 16 rows name the same one
- model_bus: int32 [16384], P(('net', 'dev')), may hold values from 0 to 4095
- line_from: int32 [16384], P('net'), may hold values from 0 to 4095
- line_to: int32 [16384], P('net'), may hold values from 0 to 4095
- line_delay: int32 [16384], P('net'), may hold values from 2 to 6
- line_imped: float32 [16384], P('net'), may hold values from 2 to 8
- wave_from_past: float32 [6, 16384], P(None, 'net'), may hold values from -6 to 6
- wave_to_past: float32 [6, 16384], P(None, 'net'), may hold values from -6 to 6
Outputs:
- voltage_trace: float32 [8, 131072], P(None, 'net')
- final_state: float32 [16384, 128], P(('net', 'dev'))
Inputs may be any that keep to these rules, and one draw needn't show every extreme that they name: `model_owner`: among the models of one device (aligned blocks of 128 rows) at most 16 name the same owner, a bound that some block reaches.
All inputs are finite; a program needn't handle non-finite values.
Results may differ from a plain program's by a relative error of at most 0.0003.
Values sent between devices are 32-bit elements; how exact they have to be, the bound alone decides.
A program may use at most 128 MiB of HBM per device.

v0:
```python
import jax
import jax.numpy as jnp
from jax import lax
from jax.sharding import PartitionSpec as P

STEPS = 8
DMAX = 6


def from_behind(array, axis, by):
    devices = lax.axis_size(axis)
    return lax.ppermute(array, axis, [(i, (i + by) % devices) for i in range(devices)])


def body(
    zinv,
    source,
    model_state,
    propagator,
    input_gain,
    output_gain,
    model_owner,
    model_bus,
    line_from,
    line_to,
    line_delay,
    line_imped,
    wave_from_past,
    wave_to_past,
):
    net_count = lax.axis_size("net")
    models_here = model_state.shape[0]
    capacity = 4 * models_here // net_count
    bus_here = source.shape[0]
    lines_here = line_from.shape[0]
    subs_here = zinv.shape[0]
    owner_net = model_owner[:, 0]
    onehot = (owner_net[:, None] == jnp.arange(net_count, dtype=jnp.int32)[None, :]).astype(
        jnp.int32
    )
    running = jnp.cumsum(onehot, 0)
    ranking = jnp.sum(onehot * (running - 1), 1)
    slot_index = owner_net * capacity + ranking
    send_ids = jnp.full((net_count * capacity,), bus_here, jnp.int32).at[slot_index].set(model_bus)
    asked_ids = lax.all_to_all(
        send_ids.reshape(net_count, capacity), "net", split_axis=0, concat_axis=0, tiled=True
    ).reshape(-1)
    global_bus = owner_net * bus_here + model_bus
    to_here = from_behind(line_to, "net", 1)
    block_len = 1
    from_waves = jnp.zeros((DMAX + STEPS, lines_here), jnp.float32).at[:DMAX].set(wave_from_past)
    to_waves = jnp.zeros((DMAX + STEPS, lines_here), jnp.float32).at[:DMAX].set(wave_to_past)
    state = model_state
    traces = []
    for block_start in range(0, STEPS, block_len):
        moments = list(range(block_start, block_start + block_len))
        arrivals_from = []
        arrivals_to = []
        for moment in moments:
            lookback = moment + DMAX - line_delay
            arrivals_from.append(jnp.take_along_axis(to_waves, lookback[None, :], 0)[0])
            arrivals_to.append(jnp.take_along_axis(from_waves, lookback[None, :], 0)[0])
        incoming = from_behind(jnp.stack(arrivals_to), "net", 1)
        volts_list = []
        for offset, moment in enumerate(moments):
            currents = jnp.sum(state * output_gain, 1)
            outgoing = jnp.zeros((net_count * capacity,), jnp.float32).at[slot_index].set(currents)
            line_inj = (
                jnp.zeros((bus_here,), jnp.float32)
                .at[line_from]
                .add(arrivals_from[offset])
                .at[to_here]
                .add(incoming[offset])
            )
            received = lax.all_to_all(
                outgoing.reshape(net_count, capacity),
                "net",
                split_axis=0,
                concat_axis=0,
                tiled=True,
            ).reshape(-1)
            partial_value = (
                jnp.zeros((bus_here,), jnp.float32).at[asked_ids].add(received, mode="drop")
            )
            model_inj = lax.psum(partial_value, "dev")
            injection = source + model_inj + line_inj
            rows_part = jnp.einsum(
                "sij,sj->si",
                zinv,
                injection.reshape(subs_here, -1),
                precision=lax.Precision.HIGHEST,
            )
            volts = lax.all_gather(rows_part, "dev", axis=1, tiled=True).reshape(bus_here)
            volts_list.append(volts)
            every_volt = lax.all_gather(volts, "net", axis=0, tiled=True)
            model_volts = every_volt[global_bus]
            state = (
                jnp.einsum("ms,mst->mt", state, propagator, precision=lax.Precision.HIGHEST)
                + model_volts[:, None] * input_gain
            )
        far_list = []
        for offset, moment in enumerate(moments):
            volts = volts_list[offset]
            from_waves = from_waves.at[DMAX + moment].set(
                2.0 * volts[line_from] / line_imped - arrivals_from[offset]
            )
            far_list.append(volts[to_here])
            traces.append(volts)
        far_volts = from_behind(jnp.stack(far_list), "net", -1)
        for offset, moment in enumerate(moments):
            to_waves = to_waves.at[DMAX + moment].set(
                2.0 * far_volts[offset] / line_imped - arrivals_to[offset]
            )
    return (jnp.stack(traces), state)


def solution(mesh):
    in_specs = (
        P("net", "dev", None),
        P("net"),
        P(("net", "dev"), None),
        P(("net", "dev"), None, None),
        P(("net", "dev"), None),
        P(("net", "dev"), None),
        P(("net", "dev"), None),
        P(("net", "dev")),
        P("net"),
        P("net"),
        P("net"),
        P("net"),
        P(None, "net"),
        P(None, "net"),
    )
    out_specs = (P(None, "net"), P(("net", "dev"), None))
    return jax.shard_map(body, mesh=mesh, in_specs=in_specs, out_specs=out_specs, check_vma=False)
```

profile of v0, /device:TPU:1, one launch (start us, length us, event | category | flops | bytes accessed | tf_op | source)
XLA Modules:
  0.0 852.0 jit_solution(3217291244234894855)
XLA Ops:
  29.1 9.4 %fusion.77 = f32[128,1,128]{2,1,0:T(1,128)S(1)} fusion(f32[128,128,1]{1,2,0:T(1,128)} %bitcast.363, f32[128,128,128]{2,1,0:T(8,128)} %param.51), kind=kOutput, calls=%fused_computation.276 | convolution fusion | flops 25165824 | bytes 8519680 | tf_op jit(solution)/shard_map/ms,mst->mt/dot_general | solution.py:98
  58.6 14.4 %psum.56 = f32[4096]{0:T(1024)S(1)} all-reduce(f32[4096]{0:T(1024)S(1)} %scatter_custom_fusion.2), channel_id=1, replica_groups=mesh['net'=32,'dev'=4] {'dev'}, use_global_device_ids=true, to_apply=%region_6.7 | all-reduce | flops 4096 | bytes 32768 | tf_op jit(solution)/shard_map/psum | solution.py:85
  94.8 30.0 %all_gather.49 = f32[131072]{0:T(1024)S(1)} all-gather(f32[4096]{0:T(1024)S(1)} %bitcast.328), channel_id=1, replica_groups=mesh['net'=32,'dev'=4] {'net'}, dimensions={0}, use_global_device_ids=true | all-gather | bytes 540672 | tf_op jit(solution)/shard_map/all_gather | solution.py:95
  137.9 9.4 %fusion.79 = f32[128,1,128]{2,1,0:T(1,128)S(1)} fusion(f32[128,128,1]{1,2,0:T(1,128)S(1)} %bitcast.372, f32[128,128,128]{2,1,0:T(8,128)} %param.51), kind=kOutput, calls=%fused_computation.278 | convolution fusion | flops 25165824 | bytes 8519680 | tf_op jit(solution)/shard_map/ms,mst->mt/dot_general | solution.py:98
  165.6 11.0 %psum.57 = f32[4096]{0:T(1024)S(1)} all-reduce(f32[4096]{0:T(1024)S(1)} %scatter_custom_fusion.6), channel_id=1, replica_groups=mesh['net'=32,'dev'=4] {'dev'}, use_global_device_ids=true, to_apply=%region_12.14 | all-reduce | flops 4096 | bytes 32768 | tf_op jit(solution)/shard_map/psum | solution.py:85
  201.3 29.9 %all_gather.51 = f32[131072]{0:T(1024)S(1)} all-gather(f32[4096]{0:T(1024)S(1)} %bitcast.332), channel_id=1, replica_groups=mesh['net'=32,'dev'=4] {'net'}, dimensions={0}, use_global_device_ids=true | all-gather | bytes 540672 | tf_op jit(solution)/shard_map/all_gather | solution.py:95
  240.6 9.4 %fusion.81 = f32[128,1,128]{2,1,0:T(1,128)S(1)} fusion(f32[128,128,1]{1,2,0:T(1,128)S(1)} %bitcast.373, f32[128,128,128]{2,1,0:T(8,128)} %param.51), kind=kOutput, calls=%fused_computation.280 | convolution fusion | flops 25165824 | bytes 8519680 | tf_op jit(solution)/shard_map/ms,mst->mt/dot_general | solution.py:98
  268.4 11.6 %psum.58 = f32[4096]{0:T(1024)S(1)} all-reduce(f32[4096]{0:T(1024)S(1)} %scatter_custom_fusion.10), channel_id=1, replica_groups=mesh['net'=32,'dev'=4] {'dev'}, use_global_device_ids=true, to_apply=%region_18.20 | all-reduce | flops 4096 | bytes 32768 | tf_op jit(solution)/shard_map/psum | solution.py:85
  304.7 30.4 %all_gather.53 = f32[131072]{0:T(1024)S(1)} all-gather(f32[4096]{0:T(1024)S(1)} %bitcast.335), channel_id=1, replica_groups=mesh['net'=32,'dev'=4] {'net'}, dimensions={0}, use_global_device_ids=true | all-gather | bytes 540672 | tf_op jit(solution)/shard_map/all_gather | solution.py:95
  344.9 9.4 %fusion.83 = f32[128,1,128]{2,1,0:T(1,128)S(1)} fusion(f32[128,128,1]{1,2,0:T(1,128)S(1)} %bitcast.374, f32[128,128,128]{2,1,0:T(8,128)} %param.51), kind=kOutput, calls=%fused_computation.282 | convolution fusion | flops 25165824 | bytes 8519680 | tf_op jit(solution)/shard_map/ms,mst->mt/dot_general | solution.py:98
  372.6 11.0 %psum.59 = f32[4096]{0:T(1024)S(1)} all-reduce(f32[4096]{0:T(1024)S(1)} %scatter_custom_fusion.14), channel_id=1, replica_groups=mesh['net'=32,'dev'=4] {'dev'}, use_global_device_ids=true, to_apply=%region_24.26 | all-reduce | flops 4096 | bytes 32768 | tf_op jit(solution)/shard_map/psum | solution.py:85
  408.3 29.9 %all_gather.55 = f32[131072]{0:T(1024)S(1)} all-gather(f32[4096]{0:T(1024)S(1)} %bitcast.338), channel_id=1, replica_groups=mesh['net'=32,'dev'=4] {'net'}, dimensions={0}, use_global_device_ids=true | all-gather | bytes 540672 | tf_op jit(solution)/shard_map/all_gather | solution.py:95
  447.6 9.4 %fusion.85 = f32[128,1,128]{2,1,0:T(1,128)S(1)} fusion(f32[128,128,1]{1,2,0:T(1,128)S(1)} %bitcast.375, f32[128,128,128]{2,1,0:T(8,128)} %param.51), kind=kOutput, calls=%fused_computation.284 | convolution fusion | flops 25165824 | bytes 8519680 | tf_op jit(solution)/shard_map/ms,mst->mt/dot_general | solution.py:98
  475.4 11.6 %psum.60 = f32[4096]{0:T(1024)S(1)} all-reduce(f32[4096]{0:T(1024)S(1)} %scatter_custom_fusion.18), channel_id=1, replica_groups=mesh['net'=32,'dev'=4] {'dev'}, use_global_device_ids=true, to_apply=%region_30.32 | all-reduce | flops 4096 | bytes 32768 | tf_op jit(solution)/shard_map/psum | solution.py:85
  511.6 30.4 %all_gather.57 = f32[131072]{0:T(1024)S(1)} all-gather(f32[4096]{0:T(1024)S(1)} %bitcast.341), channel_id=1, replica_groups=mesh['net'=32,'dev'=4] {'net'}, dimensions={0}, use_global_device_ids=true | all-gather | bytes 540672 | tf_op jit(solution)/shard_map/all_gather | solution.py:95
  551.9 9.4 %fusion.87 = f32[128,1,128]{2,1,0:T(1,128)S(1)} fusion(f32[128,128,1]{1,2,0:T(1,128)S(1)} %bitcast.376, f32[128,128,128]{2,1,0:T(8,128)} %param.51), kind=kOutput, calls=%fused_computation.286 | convolution fusion | flops 25165824 | bytes 8519680 | tf_op jit(solution)/shard_map/ms,mst->mt/dot_general | solution.py:98
  579.5 11.0 %psum.61 = f32[4096]{0:T(1024)S(1)} all-reduce(f32[4096]{0:T(1024)S(1)} %scatter_custom_fusion.22), channel_id=1, replica_groups=mesh['net'=32,'dev'=4] {'dev'}, use_global_device_ids=true, to_apply=%region_36.38 | all-reduce | flops 4096 | bytes 32768 | tf_op jit(solution)/shard_map/psum | solution.py:85
  615.3 29.9 %all_gather.59 = f32[131072]{0:T(1024)S(1)} all-gather(f32[4096]{0:T(1024)S(1)} %bitcast.344), channel_id=1, replica_groups=mesh['net'=32,'dev'=4] {'net'}, dimensions={0}, use_global_device_ids=true | all-gather | bytes 540672 | tf_op jit(solution)/shard_map/all_gather | solution.py:95
  654.5 9.4 %fusion.89 = f32[128,1,128]{2,1,0:T(1,128)S(1)} fusion(f32[128,128,1]{1,2,0:T(1,128)S(1)} %bitcast.377, f32[128,128,128]{2,1,0:T(8,128)} %param.51), kind=kOutput, calls=%fused_computation.288 | convolution fusion | flops 25165824 | bytes 8519680 | tf_op jit(solution)/shard_map/ms,mst->mt/dot_general | solution.py:98
  682.4 11.6 %psum.62 = f32[4096]{0:T(1024)S(1)} all-reduce(f32[4096]{0:T(1024)S(1)} %scatter_custom_fusion.26), channel_id=1, replica_groups=mesh['net'=32,'dev'=4] {'dev'}, use_global_device_ids=true, to_apply=%region_42.44 | all-reduce | flops 4096 | bytes 32768 | tf_op jit(solution)/shard_map/psum | solution.py:85
  718.6 30.4 %all_gather.61 = f32[131072]{0:T(1024)S(1)} all-gather(f32[4096]{0:T(1024)S(1)} %bitcast.326), channel_id=1, replica_groups=mesh['net'=32,'dev'=4] {'net'}, dimensions={0}, use_global_device_ids=true | all-gather | bytes 540672 | tf_op jit(solution)/shard_map/all_gather | solution.py:95
  758.8 9.4 %fusion.91 = f32[128,1,128]{2,1,0:T(1,128)S(1)} fusion(f32[128,128,1]{1,2,0:T(1,128)S(1)} %bitcast.371, f32[128,128,128]{2,1,0:T(8,128)} %param.51), kind=kOutput, calls=%fused_computation.290 | convolution fusion | flops 25165824 | bytes 8519680 | tf_op jit(solution)/shard_map/ms,mst->mt/dot_general | solution.py:98
  786.5 11.0 %psum.63 = f32[4096]{0:T(1024)S(1)} all-reduce(f32[4096]{0:T(1024)S(1)} %scatter_custom_fusion.30), channel_id=1, replica_groups=mesh['net'=32,'dev'=4] {'dev'}, use_global_device_ids=true, to_apply=%region_48.50 | all-reduce | flops 4096 | bytes 32768 | tf_op jit(solution)/shard_map/psum | solution.py:85
  819.1 29.9 %all_gather.63 = f32[131072]{0:T(1024)S(1)} all-gather(f32[4096]{0:T(1024)S(1)} %bitcast.402), channel_id=1, replica_groups=mesh['net'=32,'dev'=4] {'net'}, dimensions={0}, use_global_device_ids=true | all-gather | bytes 540672 | tf_op jit(solution)/shard_map/all_gather | solution.py:95
  (280 shorter events, 440.0 us)
Async XLA Ops:
  4.9 35.4 %all-to-all-start = ((s32[32,1,16]{2,1,0:T(1,128)}), s32[32,1,16]{2,1,0:T(1,128)S(1)}, u32[]{:S(2)}, u32[]{:S(2)}) async-start(s32[32,1,16]{2,1,0:T(1,128)} %bitcast.3), calls=%async_computation | async-start | bytes 32768 | tf_op jit(solution)/shard_map/all_to_all | solution.py:45
  24.9 51.5 %collective-permute-start.1 = (f32[1,512]{1,0:T(1,128)S(1)}, f32[1,512]{1,0:T(1,128)S(1)}, u32[]{:S(2)}, u32[]{:S(2)}) collective-permute-start(f32[1,512]{1,0:T(1,128)S(1)} %get-tuple-element.253), channel_id=1, source_target_pairs={{0,4},{4,8},{8,12},{12,16},{16,20},{20,24},{24,28},{28,32},{32,36}... | collective-permute-start | bytes 6152 | tf_op jit(solution)/shard_map/ppermute | solution.py:12
  26.6 49.8 %collective-permute-start = (s32[512]{0:T(512)}, s32[512]{0:T(512)S(1)}, u32[]{:S(2)}, u32[]{:S(2)}) collective-permute-start(s32[512]{0:T(512)} %param.57), channel_id=1, source_target_pairs={{0,4},{4,8},{8,12},{12,16},{16,20},{20,24},{24,28},{28,32},{32,36}... | collective-permute-start | bytes 6152 | tf_op jit(solution)/shard_map/ppermute | solution.py:12
  127.9 26.6 %collective-permute-start.2 = (f32[1,512]{1,0:T(1,128)S(1)}, f32[1,512]{1,0:T(1,128)S(1)}, u32[]{:S(2)}, u32[]{:S(2)}) collective-permute-start(f32[1,512]{1,0:T(1,128)S(1)} %bitcast.510), channel_id=1, source_target_pairs={{0,124},{4,0},{8,4},{12,8},{16,12},{20,16},{24,20},{28,24},{32,28}... | collective-permute-start | bytes 6152 | tf_op jit(solution)/shard_map/ppermute | solution.py:12
  131.2 19.3 %all-to-all-start.2 = ((f32[32,1,16]{2,1,0:T(1,128)}), f32[32,1,16]{2,1,0:T(1,128)S(1)}, u32[]{:S(2)}, u32[]{:S(2)}) async-start(f32[32,1,16]{2,1,0:T(1,128)} %bitcast.23), calls=%async_computation.2 | async-start | bytes 32768 | tf_op jit(solution)/shard_map/all_to_all | solution.py:75
  163.9 16.1 %collective-permute-start.3 = (f32[1,512]{1,0:T(1,128)S(1)}, f32[1,512]{1,0:T(1,128)S(1)}, u32[]{:S(2)}, u32[]{:S(2)}) collective-permute-start(f32[1,512]{1,0:T(1,128)S(1)} %get-tuple-element.249), channel_id=1, source_target_pairs={{0,4},{4,8},{8,12},{12,16},{16,20},{20,24},{24,28},{28,32},{32,36}... | collective-permute-start | bytes 6152 | tf_op jit(solution)/shard_map/ppermute | solution.py:12
  231.3 25.9 %collective-permute-start.4 = (f32[1,512]{1,0:T(1,128)S(1)}, f32[1,512]{1,0:T(1,128)S(1)}, u32[]{:S(2)}, u32[]{:S(2)}) collective-permute-start(f32[1,512]{1,0:T(1,128)S(1)} %bitcast.505), channel_id=1, source_target_pairs={{0,124},{4,0},{8,4},{12,8},{16,12},{20,16},{24,20},{28,24},{32,28}... | collective-permute-start | bytes 6152 | tf_op jit(solution)/shard_map/ppermute | solution.py:12
  234.5 18.7 %all-to-all-start.3 = ((f32[32,1,16]{2,1,0:T(1,128)}), f32[32,1,16]{2,1,0:T(1,128)S(1)}, u32[]{:S(2)}, u32[]{:S(2)}) async-start(f32[32,1,16]{2,1,0:T(1,128)} %bitcast.46), calls=%async_computation.3 | async-start | bytes 32768 | tf_op jit(solution)/shard_map/all_to_all | solution.py:75
  266.7 16.7 %collective-permute-start.5 = (f32[1,512]{1,0:T(1,128)S(1)}, f32[1,512]{1,0:T(1,128)S(1)}, u32[]{:S(2)}, u32[]{:S(2)}) collective-permute-start(f32[1,512]{1,0:T(1,128)S(1)} %get-tuple-element.245), channel_id=1, source_target_pairs={{0,4},{4,8},{8,12},{12,16},{16,20},{20,24},{24,28},{28,32},{32,36}... | collective-permute-start | bytes 6152 | tf_op jit(solution)/shard_map/ppermute | solution.py:12
  335.1 26.4 %collective-permute-start.6 = (f32[1,512]{1,0:T(1,128)S(1)}, f32[1,512]{1,0:T(1,128)S(1)}, u32[]{:S(2)}, u32[]{:S(2)}) collective-permute-start(f32[1,512]{1,0:T(1,128)S(1)} %bitcast.506), channel_id=1, source_target_pairs={{0,124},{4,0},{8,4},{12,8},{16,12},{20,16},{24,20},{28,24},{32,28}... | collective-permute-start | bytes 6152 | tf_op jit(solution)/shard_map/ppermute | solution.py:12
  338.3 19.2 %all-to-all-start.4 = ((f32[32,1,16]{2,1,0:T(1,128)}), f32[32,1,16]{2,1,0:T(1,128)S(1)}, u32[]{:S(2)}, u32[]{:S(2)}) async-start(f32[32,1,16]{2,1,0:T(1,128)} %bitcast.69), calls=%async_computation.4 | async-start | bytes 32768 | tf_op jit(solution)/shard_map/all_to_all | solution.py:75
  370.8 16.1 %collective-permute-start.7 = (f32[1,512]{1,0:T(1,128)S(1)}, f32[1,512]{1,0:T(1,128)S(1)}, u32[]{:S(2)}, u32[]{:S(2)}) collective-permute-start(f32[1,512]{1,0:T(1,128)S(1)} %get-tuple-element.241), channel_id=1, source_target_pairs={{0,4},{4,8},{8,12},{12,16},{16,20},{20,24},{24,28},{28,32},{32,36}... | collective-permute-start | bytes 6152 | tf_op jit(solution)/shard_map/ppermute | solution.py:12
  438.3 25.9 %collective-permute-start.8 = (f32[1,512]{1,0:T(1,128)S(1)}, f32[1,512]{1,0:T(1,128)S(1)}, u32[]{:S(2)}, u32[]{:S(2)}) collective-permute-start(f32[1,512]{1,0:T(1,128)S(1)} %bitcast.507), channel_id=1, source_target_pairs={{0,124},{4,0},{8,4},{12,8},{16,12},{20,16},{24,20},{28,24},{32,28}... | collective-permute-start | bytes 6152 | tf_op jit(solution)/shard_map/ppermute | solution.py:12
  441.4 18.7 %all-to-all-start.5 = ((f32[32,1,16]{2,1,0:T(1,128)}), f32[32,1,16]{2,1,0:T(1,128)S(1)}, u32[]{:S(2)}, u32[]{:S(2)}) async-start(f32[32,1,16]{2,1,0:T(1,128)} %bitcast.92), calls=%async_computation.5 | async-start | bytes 32768 | tf_op jit(solution)/shard_map/all_to_all | solution.py:75
  473.7 16.7 %collective-permute-start.9 = (f32[1,512]{1,0:T(1,128)S(1)}, f32[1,512]{1,0:T(1,128)S(1)}, u32[]{:S(2)}, u32[]{:S(2)}) collective-permute-start(f32[1,512]{1,0:T(1,128)S(1)} %get-tuple-element.237), channel_id=1, source_target_pairs={{0,4},{4,8},{8,12},{12,16},{16,20},{20,24},{24,28},{28,32},{32,36}... | collective-permute-start | bytes 6152 | tf_op jit(solution)/shard_map/ppermute | solution.py:12
  542.1 26.4 %collective-permute-start.10 = (f32[1,512]{1,0:T(1,128)S(1)}, f32[1,512]{1,0:T(1,128)S(1)}, u32[]{:S(2)}, u32[]{:S(2)}) collective-permute-start(f32[1,512]{1,0:T(1,128)S(1)} %bitcast.508), channel_id=1, source_target_pairs={{0,124},{4,0},{8,4},{12,8},{16,12},{20,16},{24,20},{28,24},{32,28}... | collective-permute-start | bytes 6152 | tf_op jit(solution)/shard_map/ppermute | solution.py:12
  545.2 19.2 %all-to-all-start.6 = ((f32[32,1,16]{2,1,0:T(1,128)}), f32[32,1,16]{2,1,0:T(1,128)S(1)}, u32[]{:S(2)}, u32[]{:S(2)}) async-start(f32[32,1,16]{2,1,0:T(1,128)} %bitcast.115), calls=%async_computation.6 | async-start | bytes 32768 | tf_op jit(solution)/shard_map/all_to_all | solution.py:75
  577.8 16.1 %collective-permute-start.11 = (f32[1,512]{1,0:T(1,128)S(1)}, f32[1,512]{1,0:T(1,128)S(1)}, u32[]{:S(2)}, u32[]{:S(2)}) collective-permute-start(f32[1,512]{1,0:T(1,128)S(1)} %get-tuple-element.233), channel_id=1, source_target_pairs={{0,4},{4,8},{8,12},{12,16},{16,20},{20,24},{24,28},{28,32},{32,36}... | collective-permute-start | bytes 6152 | tf_op jit(solution)/shard_map/ppermute | solution.py:12
  645.2 25.9 %collective-permute-start.12 = (f32[1,512]{1,0:T(1,128)S(1)}, f32[1,512]{1,0:T(1,128)S(1)}, u32[]{:S(2)}, u32[]{:S(2)}) collective-permute-start(f32[1,512]{1,0:T(1,128)S(1)} %bitcast.509), channel_id=1, source_target_pairs={{0,124},{4,0},{8,4},{12,8},{16,12},{20,16},{24,20},{28,24},{32,28}... | collective-permute-start | bytes 6152 | tf_op jit(solution)/shard_map/ppermute | solution.py:12
  648.4 18.7 %all-to-all-start.7 = ((f32[32,1,16]{2,1,0:T(1,128)}), f32[32,1,16]{2,1,0:T(1,128)S(1)}, u32[]{:S(2)}, u32[]{:S(2)}) async-start(f32[32,1,16]{2,1,0:T(1,128)} %bitcast.138), calls=%async_computation.7 | async-start | bytes 32768 | tf_op jit(solution)/shard_map/all_to_all | solution.py:75
  680.7 16.7 %collective-permute-start.13 = (f32[1,512]{1,0:T(1,128)S(1)}, f32[1,512]{1,0:T(1,128)S(1)}, u32[]{:S(2)}, u32[]{:S(2)}) collective-permute-start(f32[1,512]{1,0:T(1,128)S(1)} %get-tuple-element.229), channel_id=1, source_target_pairs={{0,4},{4,8},{8,12},{12,16},{16,20},{20,24},{24,28},{28,32},{32,36}... | collective-permute-start | bytes 6152 | tf_op jit(solution)/shard_map/ppermute | solution.py:12
  749.0 26.4 %collective-permute-start.14 = (f32[1,512]{1,0:T(1,128)S(1)}, f32[1,512]{1,0:T(1,128)S(1)}, u32[]{:S(2)}, u32[]{:S(2)}) collective-permute-start(f32[1,512]{1,0:T(1,128)S(1)} %bitcast.504), channel_id=1, source_target_pairs={{0,124},{4,0},{8,4},{12,8},{16,12},{20,16},{24,20},{28,24},{32,28}... | collective-permute-start | bytes 6152 | tf_op jit(solution)/shard_map/ppermute | solution.py:12
  752.2 19.2 %all-to-all-start.8 = ((f32[32,1,16]{2,1,0:T(1,128)}), f32[32,1,16]{2,1,0:T(1,128)S(1)}, u32[]{:S(2)}, u32[]{:S(2)}) async-start(f32[32,1,16]{2,1,0:T(1,128)} %bitcast.161), calls=%async_computation.8 | async-start | bytes 32768 | tf_op jit(solution)/shard_map/all_to_all | solution.py:75
  784.8 16.1 %collective-permute-start.15 = (f32[1,512]{1,0:T(1,128)S(1)}, f32[1,512]{1,0:T(1,128)S(1)}, u32[]{:S(2)}, u32[]{:S(2)}) collective-permute-start(f32[1,512]{1,0:T(1,128)S(1)} %get-tuple-element.209), channel_id=1, source_target_pairs={{0,4},{4,8},{8,12},{12,16},{16,20},{20,24},{24,28},{28,32},{32,36}... | collective-permute-start | bytes 6152 | tf_op jit(solution)/shard_map/ppermute | solution.py:12
  (5 other events, 342.4 us)
where the time goes:
time: 861 us; the launch traced here: 852 us
  blocking collectives  407 us (47%)
  local copies, waits for them, and re-layouts  147 us (17%)
  matrix products  121 us (14%)
  other arithmetic  94.4 us (11%)
  starting transfers between devices  75.5 us (9%)
    all_gather x8, blocking collectives, body(): every_volt = lax.all_gather(volts, 'net', axis=0, tiled=True)  241 us
    psum x8, blocking collectives, body(): model_inj = lax.psum(partial_value, 'dev')  93.4 us
    dot_general x8, matrix products, body(): jnp.einsum('ms,mst->mt', state, propagator, precision=lax.Precision.HIGHEST)  75.2 us
    all_gather x8, blocking collectives, body(): lax.all_gather(rows_part, 'dev', axis=1, tiled=True).reshape(bus_here)  72.4 us
    scatter-add x16, other arithmetic, body(): line_inj = jnp.zeros((bus_here,), jnp.float32).at[line_from].add(arrivals...  54.4 us
    all_to_all x8, starting transfers between devices, body(): lax.all_to_all(outgoing.reshape(net_count, capacity), 'net', split_axis=0...  51.9 us
    dot_general x8, matrix products, body(): jnp.einsum('sij,sj->si', zinv, injection.reshape(subs_here, -1), precisio...  45.3 us
    gather x8, local copies, waits for them, and re-layouts, body(): arrivals_from.append(jnp.take_along_axis(to_waves, lookback[None, :], 0)[0])  36.4 us
  transfers between devices with their start and end apart: 25, of which 1 were waited for; matrix products, arithmetic and copies ran while one was open for 22% of the time, Pallas kernels for 0%

commit v1 on v0

v1 whole, which is shorter than its diff:
```python
import functools
import jax
import jax.numpy as jnp
from jax import lax
from jax.experimental import pallas as pl
from jax.experimental.pallas import tpu as pltpu
from jax.sharding import PartitionSpec as P

STEPS = 8
DMIN = 2
DMAX = 6
NETS = 32
DEVS = 4
CAP = 16
F32 = jnp.float32
BF16 = jnp.bfloat16
MESH = pl.DeviceIdType.MESH


def rows_sum(x):
    return jnp.sum(x, axis=0, keepdims=True)


def parts(x, count=3):
    pieces = []
    for i in range(count):
        piece = x.astype(BF16)
        pieces.append(piece)
        if i + 1 < count:
            x = x - piece.astype(F32)
    return pieces


def dot(a, b, dims):
    return lax.dot_general(a, b, (dims, ((), ())), preferred_element_type=F32)


def nn(a, b):
    return dot(a, b, ((1,), (0,)))


def nt(a, b):
    return dot(a, b, ((1,), (1,)))


def tn(a, b):
    return dot(a, b, ((0,), (0,)))


def iota(shape, dim):
    return lax.broadcasted_iota(jnp.int32, shape, dim)


def iota_f(shape, dim):
    return iota(shape, dim).astype(F32)


def one(mask):
    return jnp.where(mask, 1.0, 0.0).astype(F32)


def third_sum(x):
    rows = x.shape[0] // 3
    return x[:rows] + x[rows:2 * rows] + x[2 * rows:]


def grid_kernel(z, src, lines, mod, fh, xb, trace, final,
                asend, arecv, vall, uv, prev, wsend, wrecv, rsend, rrecv, ohl, ohs,
                a_s, a_r, v_s, v_r, uv_s, uv_r, w_s, w_r, l_s, l_r, r_s, r_r):
    n = lax.axis_index("net")
    d = lax.axis_index("dev")

    def net(k):
        return lax.rem(n + k, NETS)

    def dev(j):
        return lax.rem(d + j, DEVS)

    def copy(a, b, send, recv, to_net, to_dev):
        return pltpu.make_async_remote_copy(src_ref=a, dst_ref=b, send_sem=send, recv_sem=recv,
                                            device_id=(to_net, to_dev), device_id_type=MESH)

    bar = pltpu.get_barrier_semaphore()

    def greet(to_net, to_dev):
        pl.semaphore_signal(bar, inc=1, device_id=(to_net, to_dev), device_id_type=MESH)

    lax.fori_loop(1, NETS, lambda k, _: (greet(net(k), d), 0)[1], 0)
    for j in range(1, DEVS):
        greet(n, dev(j))
        greet(net(1), dev(j))
        greet(net(NETS - 1), dev(j))
    pl.semaphore_wait(bar, NETS - 1 + 3 * (DEVS - 1))

    line_copy = copy(lines, prev, l_s, l_r, net(1), d)
    line_copy.start()

    owner = mod[0:1, :]
    offset = owner - n.astype(F32)
    offset = jnp.where(offset < 0.0, offset + float(NETS), offset)
    wide = jnp.broadcast_to(owner, (128, 128))
    earlier = one(wide.T == wide) * one(iota((128, 128), 0) < iota((128, 128), 1))
    rank = rows_sum(earlier)
    own = one(iota_f((NETS, 128), 0) == offset)
    own_b = own.astype(BF16)
    seat = one(iota_f((CAP, 128), 0) == rank)
    values = [fh[q:q + 1, :] for q in range(15)] + [mod[1:2, :] + 1.0]
    table = jnp.concatenate([value * seat for value in values], axis=0)
    packed = sum(nt(own_b, piece) for piece in parts(table))
    asend[:, 0, :] = packed
    arecv[0] = packed[0:1, :]

    def a_copy(k):
        return copy(asend.at[k], arecv.at[k], a_s.at[k], a_r.at[k], net(k), d)

    lax.fori_loop(1, NETS, lambda k, _: (a_copy(k).start(), 0)[1], 0)

    line_copy.wait_recv()
    ends = jnp.concatenate([lines[9:10, :], prev[0:1, :]], axis=1)
    delay = jnp.concatenate([lines[1:2, :], prev[1:2, :]], axis=1)
    twice = 2.0 / jnp.concatenate([lines[2:3, :], prev[2:3, :]], axis=1)
    waves = [jnp.concatenate([lines[10 + i:11 + i, :], prev[3 + i:4 + i, :]], axis=1) for i in range(DMAX)]
    high = jnp.floor(ends * (1.0 / 128.0))
    low = ends - 128.0 * high
    row = iota((8, 1), 0)
    row_high = ((row // 2) * 8 + 2 * d + row % 2).astype(F32)
    end_row = one(high == row_high)
    mine = rows_sum(end_row)
    ohl[...] = one(iota_f((128, 1024), 0) == low).astype(BF16)

    def arrivals(t):
        got = jnp.zeros((1, 1024), F32)
        for lag in range(DMIN, DMAX + 1):
            if DMAX + t - lag < len(waves):
                got = jnp.where(delay == float(lag), waves[DMAX + t - lag], got)
        return got

    def inject(arrive):
        pieces = jnp.concatenate(parts(end_row * arrive), axis=0)
        return third_sum(nt(pieces, ohl[...]))

    def sample(volts):
        pieces = jnp.concatenate(parts(volts), axis=0)
        return rows_sum(third_sum(nn(pieces, ohl[...])) * end_row)

    arrive = [arrivals(0), arrivals(1)]
    line_part = [inject(arrive[0]), inject(arrive[1])]

    seat_mask = one(iota((CAP, 256), 1) % CAP == iota((CAP, 256), 0))
    lax.fori_loop(1, NETS, lambda k, _: (a_copy(k).wait_recv(), 0)[1], 0)
    spread = jnp.concatenate([arecv[k] * seat_mask for k in range(NETS)], axis=0)
    collect = one(iota((16, 256), 1) // CAP == iota((16, 256), 0)).astype(BF16)
    vall[d] = sum(nt(collect, piece) for piece in parts(spread))

    def v_copy(j):
        return copy(vall.at[d], vall.at[d], v_s.at[j], v_r.at[d], n, dev(j))

    def v_wait(j):
        return copy(vall.at[dev(j)], vall.at[dev(j)], v_s.at[j], v_r.at[dev(j)], n, dev(j))

    for j in range(1, DEVS):
        v_copy(j).start()
    total = jnp.zeros((360, 128), F32)
    slot_high = None
    for j in range(DEVS):
        if j:
            v_wait(j).wait_recv()
        vals = vall[dev(j)]
        bus = vals[15:16, :] - 1.0
        b_high = jnp.floor(bus * (1.0 / 128.0))
        b_low = bus - 128.0 * b_high
        hot = one(iota_f((128, 512), 0) == b_low).astype(BF16)
        if j == 0:
            slot_high = b_high
            ohs[...] = hot
        b_row = one(b_high == row_high)
        left = jnp.concatenate([vals[q:q + 1, :] * b_row for q in range(15)], axis=0)
        total = total + nt(jnp.concatenate(parts(left), axis=0), hot)
    total = third_sum(total)
    free = [total[8 * q:8 * q + 8] for q in range(8)]
    gain = [total[8 * q:8 * q + 8] for q in range(8, 15)]
    source = jnp.concatenate([src[s, d] for s in range(4)], axis=0)

    def uv_copy(t, j):
        return copy(uv.at[t, d], uv.at[t, d], uv_s.at[t, j], uv_r.at[t, d], n, dev(j))

    def uv_wait(t, j):
        return copy(uv.at[t, dev(j)], uv.at[t, dev(j)], uv_s.at[t, j], uv_r.at[t, dev(j)], n, dev(j))

    def w_copy(t, way, j):
        return copy(wsend.at[t, way], wrecv.at[t, way, d], w_s.at[t, way, j], w_r.at[t, way, d],
                    net(1 if way == 0 else NETS - 1), dev(j))

    def w_wait(t, way, j):
        return copy(wsend.at[t, way], wrecv.at[t, way, dev(j)], w_s.at[t, way, j], w_r.at[t, way, dev(j)],
                    net(1 if way == 0 else NETS - 1), dev(j))

    def solve(t):
        rows = []
        for s in range(4):
            total = None
            for c in range(8):
                term = z[s, :, 128 * c:128 * c + 128] * uv[t, c // 2, 0, 2 * s + c % 2:2 * s + c % 2 + 1, :]
                total = term if total is None else total + term
            rows.append(rows_sum(total[:128].T))
            rows.append(rows_sum(total[128:].T))
        return jnp.concatenate(rows, axis=0)

    def keep(t):
        for c in range(8):
            for s in range(4):
                at = 1024 * s + 128 * c
                trace[t:t + 1, at:at + 128] = uv[t + 1, c // 2, 1, 2 * s + c % 2:2 * s + c % 2 + 1, :]

    uv[0, d, 0] = source + free[0] + line_part[0]
    uv[0, d, 1] = jnp.zeros((8, 128), F32)
    for j in range(1, DEVS):
        uv_copy(0, j).start()
    volts = []
    for t in range(STEPS):
        for j in range(1, DEVS):
            uv_wait(t, j).wait_recv()
        v = solve(t)
        volts.append(v)
        if t + 1 < STEPS:
            if t >= 1:
                for way in range(2):
                    for j in range(DEVS):
                        w_wait(t - 1, way, j).wait_recv()
                waves.append(jnp.concatenate([sum(wrecv[t - 1, 1, j] for j in range(DEVS)),
                                              sum(wrecv[t - 1, 0, j] for j in range(DEVS))], axis=1))
                arrive.append(arrivals(t + 1))
                line_part.append(inject(arrive[t + 1]))
            u = source + free[t + 1] + line_part[t + 1]
            for k in range(t + 1):
                u = u + gain[t - k] * volts[k]
        else:
            u = jnp.zeros((8, 128), F32)
        uv[t + 1, d, 0] = u
        uv[t + 1, d, 1] = v
        for j in range(1, DEVS):
            uv_copy(t + 1, j).start()
        if t <= STEPS - 1 - DMIN:
            wave = mine * (sample(v) * twice - arrive[t])
            wsend[t, 0] = wave[:, :512]
            wsend[t, 1] = wave[:, 512:]
            for way in range(2):
                for j in range(DEVS):
                    w_copy(t, way, j).start()
        if t:
            keep(t - 1)
    for j in range(1, DEVS):
        uv_wait(STEPS, j).wait_recv()

    full = jnp.concatenate([uv[t + 1, c, 1] for t in range(STEPS) for c in range(DEVS)], axis=0)
    reached = sum(nn(piece, ohs[...]) for piece in parts(full))
    row32 = iota((32, 1), 0)
    high32 = (((row32 % 8) // 2) * 8 + 2 * (row32 // 8) + row32 % 2).astype(F32)
    pick = one(slot_high == high32)
    at_slot = [rows_sum(reached[32 * t:32 * t + 32] * pick) for t in range(STEPS)]
    seat512 = one(iota((CAP, 512), 1) % CAP == iota((CAP, 512), 0))
    home = one(iota((NETS, 512), 1) // CAP == iota((NETS, 512), 0)).astype(BF16)
    table = jnp.concatenate([x * seat512 for x in at_slot], axis=0)
    back = sum(nt(home, piece) for piece in parts(table))
    rsend[:, 0, :] = back
    rrecv[0] = back[0:1, :]

    def r_copy(k):
        return copy(rsend.at[k], rrecv.at[k], r_s.at[k], r_r.at[k], net(NETS - k), d)

    lax.fori_loop(1, NETS, lambda k, _: (r_copy(k).start(), 0)[1], 0)
    keep(STEPS - 1)

    def drain(k, _):
        a_copy(k).wait_send()
        r_copy(k).wait_send()
        r_copy(k).wait_recv()
        return 0

    lax.fori_loop(1, NETS, drain, 0)
    answer = rrecv[:, 0, :]
    at_model = sum(tn(piece, own_b) for piece in parts(answer))
    state = xb[0]
    for t in range(STEPS):
        mv = rows_sum(at_model[CAP * t:CAP * t + CAP] * seat)
        state = state + mv * xb[STEPS - t]
    final[...] = state.T

    line_copy.wait_send()
    for j in range(1, DEVS):
        v_copy(j).wait_send()
        for t in range(STEPS + 1):
            uv_copy(t, j).wait_send()
    for t in range(STEPS - DMIN):
        for way in range(2):
            for j in range(DEVS):
                w_copy(t, way, j).wait_send()


def model_kernel(prop, state, bgain, og, fh, xb, raw, at, xs, bs, sems, *, unroll):
    def cp(c):
        return pltpu.make_async_copy(prop.at[:, pl.ds(8 * c, 8), :], raw.at[c], sems.at[c])
    for c in range(16):
        cp(c).start()
    xs[...] = state[...].T
    bs[...] = bgain[...].T
    ogt = og[...].T
    fh[0:1, :] = rows_sum(xs[...] * ogt)
    fh[8:9, :] = rows_sum(bs[...] * ogt)
    fh[15:16, :] = jnp.zeros((1, 128), F32)
    xb[1] = bs[...]
    flat = raw.reshape(16, 1024, 128)

    def first(c, acc):
        cp(c).wait()
        ax, ab = acc
        for kk in range(8):
            a = flat[c, pl.ds(kk, 128, stride=8), :].T
            k = 8 * c + kk
            at[k] = a
            ax = ax + a * xs[pl.ds(k, 1), :]
            ab = ab + a * bs[pl.ds(k, 1), :]
        return ax, ab

    zero = jnp.zeros((128, 128), F32)
    ax, ab = lax.fori_loop(0, 16, first, (zero, zero))

    def later(i, acc):
        ax, ab = acc
        for kk in range(unroll):
            k = i * unroll + kk
            a = at[k]
            ax = ax + a * xs[pl.ds(k, 1), :]
            ab = ab + a * bs[pl.ds(k, 1), :]
        return ax, ab

    for it in range(1, 9):
        xs[...] = ax
        bs[...] = ab
        if it < 8:
            fh[it:it + 1, :] = rows_sum(ax * ogt)
            if it < 7:
                fh[8 + it:9 + it, :] = rows_sum(ab * ogt)
            xb[1 + it] = ab
            ax, ab = lax.fori_loop(0, 128 // unroll, later, (zero, zero))
        else:
            xb[0] = ax

def models(prop, state, bgain, og, unroll=4):
    v = pl.BlockSpec(memory_space=pltpu.VMEM)
    return pl.pallas_call(
        functools.partial(model_kernel, unroll=unroll),
        out_shape=(jax.ShapeDtypeStruct((16, 128), F32), jax.ShapeDtypeStruct((9, 128, 128), F32)),
        in_specs=[pl.BlockSpec(memory_space=pl.ANY), v, v, v],
        out_specs=(v, v),
        scratch_shapes=[pltpu.VMEM((16, 128, 8, 128), F32), pltpu.VMEM((128, 128, 128), F32),
                        pltpu.VMEM((128, 128), F32), pltpu.VMEM((128, 128), F32), pltpu.SemaphoreType.DMA((16,))],
        compiler_params=pltpu.CompilerParams(vmem_limit_bytes=40 << 20),
    )(prop, state, bgain, og)


def steps_call(z, src, lines, mod, fh, xb):
    v = pl.BlockSpec(memory_space=pltpu.VMEM)
    dma = pltpu.SemaphoreType.DMA
    return pl.pallas_call(
        grid_kernel,
        out_shape=(jax.ShapeDtypeStruct((STEPS, 4096), F32), jax.ShapeDtypeStruct((128, 128), F32)),
        in_specs=[v] * 6,
        out_specs=(v, v),
        scratch_shapes=[
            pltpu.VMEM((NETS, 1, 256), F32), pltpu.VMEM((NETS, 1, 256), F32),
            pltpu.VMEM((DEVS, 16, 512), F32), pltpu.VMEM((STEPS + 1, DEVS, 2, 8, 128), F32),
            pltpu.VMEM((16, 512), F32), pltpu.VMEM((6, 2, 1, 512), F32), pltpu.VMEM((6, 2, DEVS, 1, 512), F32),
            pltpu.VMEM((NETS, 1, 128), F32), pltpu.VMEM((NETS, 1, 128), F32),
            pltpu.VMEM((128, 1024), BF16), pltpu.VMEM((128, 512), BF16),
            dma((NETS,)), dma((NETS,)), dma((DEVS,)), dma((DEVS,)), dma((STEPS + 1, DEVS)), dma((STEPS + 1, DEVS)),
            dma((6, 2, DEVS)), dma((6, 2, DEVS)), dma, dma, dma((NETS,)), dma((NETS,)),
        ],
        compiler_params=pltpu.CompilerParams(collective_id=0, has_side_effects=True, vmem_limit_bytes=40 << 20),
    )(z, src, lines, mod, fh, xb)


def body(zinv, source, model_state, propagator, input_gain, output_gain, model_owner, model_bus,
         line_from, line_to, line_delay, line_imped, wave_from_past, wave_to_past):
    def r(x):
        return x.astype(F32)[None, :]
    lines = jnp.concatenate([r(line_to), r(line_delay), r(line_imped), wave_from_past, r(line_from), wave_to_past], axis=0)
    mod = jnp.concatenate([r(model_owner[:, 0]), r(model_bus), jnp.zeros((6, 128), F32)], axis=0)
    fh, xb = models(propagator, model_state, input_gain, output_gain)
    return steps_call(zinv, source.reshape(4, 4, 2, 128), lines, mod, fh, xb)


def solution(mesh):
    one_axis, both = P("net"), P(("net", "dev"))
    two = P(("net", "dev"), None)
    in_specs = (P("net", "dev", None), one_axis, two, P(("net", "dev"), None, None), two, two, two, both,
                one_axis, one_axis, one_axis, one_axis, P(None, "net"), P(None, "net"))
    return jax.shard_map(body, mesh=mesh, in_specs=in_specs, out_specs=(P(None, "net"), two), check_vma=False)
```

time: 861 us -> 101 us (0.12)
  blocking collectives: 407 us -> 0 us
  local copies, waits for them, and re-layouts: 147 us -> 9.52 us
  matrix products: 121 us -> 0 us
  other arithmetic: 94.4 us -> 3.44 us
  Pallas kernels: 0 us -> 86.4 us
  starting transfers between devices: 75.5 us -> 0 us
    all_gather x16 -> x0, blocking collectives: 313 us -> none  [the longest x8 241 us: body(): every_volt = lax.all_gather(volts, 'net', axis=0, tiled=True)]
    gather x38 -> x0, local copies, waits for them, and re-layouts: 126 us -> none  [the longest x8 36.4 us: body(): arrivals_from.append(jnp.take_along_axis(to_waves, lookback[None, :], 0)[0])]
    dot_general x16 -> x0, matrix products: 121 us -> none  [the longest x8 75.2 us: body(): jnp.einsum('ms,mst->mt', state, propagator, precision=lax.Precision.HIGHEST)]
    psum x8 -> x0, blocking collectives: 93.4 us -> none  [body(): model_inj = lax.psum(partial_value, 'dev')]
    pallas_call x0 -> x2, Pallas kernels: none -> 86.4 us  [the longest x1 69.9 us: steps_call(): pl.pallas_call(grid_kernel, out_shape=(jax.ShapeDtypeStruct((STEPS, 4096)...]
    scatter-add x24 -> x0, other arithmetic: 80.5 us -> none  [the longest x16 54.4 us: body(): line_inj = jnp.zeros((bus_here,), jnp.float32).at[line_from].add(arrivals...]
    all_to_all x9 -> x0, starting transfers between devices: 60.5 us -> none  [the longest x8 51.9 us: body(): lax.all_to_all(outgoing.reshape(net_count, capacity), 'net', split_axis=0...]
    ppermute x16 -> x0, starting transfers between devices: 15 us -> none  [from_behind(): lax.ppermute(array, axis, [(i, (i + by) % devices) for i in range(devices)])]
  transfers between devices with their start and end apart: 25 -> 0, of which waited for: 1 -> 0; matrix products, arithmetic and copies ran while one was open for 22% -> 0% of each run, Pallas kernels for 0% -> 0%
where the time goes in v1:
time: 101 us; the launch traced here: 100 us
  Pallas kernels  86.4 us (86%)
  local copies, waits for them, and re-layouts  9.52 us (9%)
  other arithmetic  3.44 us (3%)
    pallas_call x1, Pallas kernels, steps_call(): pl.pallas_call(grid_kernel, out_shape=(jax.ShapeDtypeStruct((STEPS, 4096)...  69.9 us
    pallas_call x1, Pallas kernels, models(): pl.pallas_call(functools.partial(model_kernel, unroll=unroll), out_shape=...  16.5 us
    unnamed x14, local copies, waits for them, and re-layouts  7.19 us
    convert_element_type x4, other arithmetic, r(): return x.astype(F32)[None, :]  2.71 us
    concatenate x1, local copies, waits for them, and re-layouts, body(): jnp.concatenate([r(line_to), r(line_delay), r(line_imped), wave_from_past...  2.25 us

profile of v1, /device:TPU:1, one launch (start us, length us, event | category | flops | bytes accessed | tf_op | source)
XLA Modules:
  0.0 100.1 jit_solution(13597709672230302744)
XLA Ops:
  0.6 0.0 copy-start.5
  0.6 0.7 convert_bitcast_fusion.1
  1.3 0.7 convert_bitcast_fusion
  2.0 0.1 pad.2.clone
  2.0 0.7 convert_element_type.27
  2.7 0.7 convert_element_type.25
  3.4 0.7 convert_element_type.26
  4.1 0.1 maximum_maximum_fusion.mod
  4.2 2.2 %concatenate.6.lines = f32[16,512]{1,0:T(8,128)S(1)} concatenate(f32[1,512]{1,0:T(1,128)S(1)} %bitcast.11, f32[1,512]{1,0:T(1,128)S(1)} %bitcast.12, f32[1,512]{1,0:T(1,128)} %bitcast.13, f32[6,512]{1,0:T(8,128)} %param.26, f32[1,512]{1,0:T(1,128)S(1)} %bitcast.10, f32[6,512]{1,0:T(8,128)} %param.27), dimensions={0} | concatenate | bytes 65536 | tf_op jit(solution)/shard_map/concatenate | solution.py:387
  6.4 0.0 copy-start
  6.4 3.4 %copy-done = f32[128,128,128]{2,1,0:T(8,128)S(1)} copy-done((f32[128,128,128]{2,1,0:T(8,128)S(1)}, f32[128,128,128]{2,1,0:T(8,128)}, u32[]{:S(2)}) %copy-start) | copy-done | bytes 8388632
  9.8 0.0 copy-start.2
  9.8 0.8 copy-done.2
  10.6 0.0 copy-start.3
  10.6 0.8 copy-done.3
  11.5 0.0 copy-start.4
  11.5 0.8 copy-done.4
  12.3 0.0 copy-start.1
  12.3 16.5 %shard_map.149 = (f32[16,128]{1,0:T(8,128)S(1)}, f32[9,128,128]{2,1,0:T(8,128)S(1)}) custom-call(f32[128,128,128]{2,1,0:T(8,128)S(1)} %copy-done, f32[128,128]{1,0:T(8,128)S(1)} %copy-done.2, f32[128,128]{1,0:T(8,128)S(1)} %copy-done.3, f32[128,128]{1,0:T(8,128)S(1)} %copy-done.4), custom_call_target="tpu_custom_call" | custom-call | tf_op jit(solution)/shard_map/pallas_call | solution.py:351
  28.8 0.0 copy-done.5
  28.8 0.0 copy-done.1
  28.8 69.9 %shard_map.150 = (f32[8,4096]{1,0:T(8,128)S(1)}, f32[128,128]{1,0:T(8,128)S(1)}) custom-call(f32[4,256,1024]{2,1,0:T(8,128)S(1)} %copy-done.1, f32[4,4,2,128]{3,2,1,0:T(2,128)S(1)} %bitcast.9, f32[16,512]{1,0:T(8,128)S(1)} %concatenate.6.lines, f32[8,128]{1,0:T(8,128)S(1)} %maximum_maximum_fusion.mod, f32[16,128]{1,0:T(8,128)S(1)} %get-tuple-element.4.fh, ...), custom_call_target="tpu_custom_call" | custom-call | tf_op jit(solution)/shard_map/pallas_call | solution.py:365
  98.8 0.7 copy.18
  99.4 0.6 copy.19
  (1 shorter events, 0.0 us)
Async XLA Ops:
  0.6 28.2 %copy-start.5 = (f32[4096]{0:T(1024)S(1)}, f32[4096]{0:T(1024)}, u32[]{:S(2)}) copy-start(f32[4096]{0:T(1024)} %param.15) | copy-start | bytes 49156
  6.4 3.4 %copy-start = (f32[128,128,128]{2,1,0:T(8,128)S(1)}, f32[128,128,128]{2,1,0:T(8,128)}, u32[]{:S(2)}) copy-start(f32[128,128,128]{2,1,0:T(8,128)} %prop.1) | copy-start | bytes 25165828
  9.8 0.8 copy-start.2
  10.6 0.8 copy-start.3
  11.5 0.8 copy-start.4
  12.3 16.5 %copy-start.1 = (f32[4,256,1024]{2,1,0:T(8,128)S(1)}, f32[4,256,1024]{2,1,0:T(8,128)}, u32[]{:S(2)}) copy-start(f32[4,256,1024]{2,1,0:T(8,128)} %z.1) | copy-start | bytes 12582916

commit v2 on v1

v2 whole, which is shorter than its diff:
```python
import jax
import jax.numpy as jnp
from jax import lax
from jax.experimental import pallas as pl
from jax.experimental.pallas import tpu as pltpu
from jax.sharding import PartitionSpec as P

STEPS = 8
DMIN = 2
DMAX = 6
NETS = 32
DEVS = 4
CAP = 16
F32 = jnp.float32
BF16 = jnp.bfloat16
MESH = pl.DeviceIdType.MESH


def rows_sum(x):
    return jnp.sum(x, axis=0, keepdims=True)


def parts(x, count=3):
    pieces = []
    for i in range(count):
        piece = x.astype(BF16)
        pieces.append(piece)
        if i + 1 < count:
            x = x - piece.astype(F32)
    return pieces


def dot(a, b, dims):
    return lax.dot_general(a, b, (dims, ((), ())), preferred_element_type=F32)


def nn(a, b):
    return dot(a, b, ((1,), (0,)))


def nt(a, b):
    return dot(a, b, ((1,), (1,)))


def tn(a, b):
    return dot(a, b, ((0,), (0,)))


def iota(shape, dim):
    return lax.broadcasted_iota(jnp.int32, shape, dim)


def iota_f(shape, dim):
    return iota(shape, dim).astype(F32)


def one(mask):
    return jnp.where(mask, 1.0, 0.0).astype(F32)


def third_sum(x):
    rows = x.shape[0] // 3
    return x[:rows] + x[rows:2 * rows] + x[2 * rows:]


def grid_kernel(zinv, source, state0, prop, bgain, ogain, owner_i, bus_i, from_i, to_i, delay_i, imped_i, fpast, tpast,
                trace, final,
                z, src, st, gi, go, own_v, bus_v, from_v, to_v, delay_v, imped_v, fp, tp,
                raw, at, xs, bs, xb, asend, arecv, vall, uv, pack, prev, wsend, wrecv, rsend, rrecv,
                ohl, hots, brow, acc, jl,
                in_s, raw_s, a_s, a_r, v_s, v_r, uv_s, uv_r, w_s, w_r, l_s, l_r, r_s, r_r):
    n = lax.axis_index("net")
    d = lax.axis_index("dev")

    def net(k):
        return lax.rem(n + k, NETS)

    def dev(j):
        return lax.rem(d + j, DEVS)

    def copy(a, b, send, recv, to_net, to_dev):
        return pltpu.make_async_remote_copy(src_ref=a, dst_ref=b, send_sem=send, recv_sem=recv,
                                            device_id=(to_net, to_dev), device_id_type=MESH)

    def others(run):
        lax.fori_loop(1, NETS, lambda k, _: (run(k), 0)[1], 0)

    pairs = [(state0, st), (bgain, gi), (ogain, go), (owner_i, own_v), (bus_i, bus_v), (from_i, from_v), (to_i, to_v),
             (delay_i, delay_v), (imped_i, imped_v), (fpast, fp), (tpast, tp), (source, src), (zinv, z)]
    loads = [pltpu.make_async_copy(a, b, in_s.at[i]) for i, (a, b) in enumerate(pairs)]

    def raw_copy(c):
        return pltpu.make_async_copy(prop.at[:, pl.ds(8 * c, 8), :], raw.at[c], raw_s.at[c])

    for load in loads[:11]:
        load.start()
    for c in range(16):
        raw_copy(c).start()
    for load in loads[11:]:
        load.start()

    bar = pltpu.get_barrier_semaphore()

    def greet(to_net, to_dev):
        pl.semaphore_signal(bar, inc=1, device_id=(to_net, to_dev), device_id_type=MESH)

    others(lambda k: greet(net(k), d))
    for j in range(1, DEVS):
        greet(n, dev(j))
        greet(net(1), dev(j))
        greet(net(NETS - 1), dev(j))

    for load in loads[:11]:
        load.wait()
    owner = own_v[...].astype(F32)
    offset = owner - n.astype(F32)
    offset = jnp.where(offset < 0.0, offset + float(NETS), offset)
    wide = jnp.broadcast_to(owner, (128, 128))
    earlier = one(wide.T == wide) * one(iota((128, 128), 0) < iota((128, 128), 1))
    rank = rows_sum(earlier)
    own = one(iota_f((NETS, 128), 0) == offset).astype(BF16)
    seat = one(iota_f((CAP, 128), 0) == rank)
    ogt = go[...].T
    go[...] = ogt
    first_x = st[...].T
    first_b = gi[...].T
    xs[...] = first_x
    bs[...] = first_b
    xb[0] = first_b
    free_m = [rows_sum(first_x * ogt)]
    gain_m = [rows_sum(first_b * ogt)]
    pack[0:1, :] = to_v[...].astype(F32)
    pack[1:2, :] = delay_v[...].astype(F32)
    pack[2:3, :] = imped_v[...]
    pack[3:9, :] = fp[...]
    pack[9:16, :] = jnp.zeros((7, 512), F32)

    flat = raw.reshape(16, 1024, 128)
    zero = jnp.zeros((128, 128), F32)

    def first(c, held):
        raw_copy(c).wait()
        ax, ab = held
        for kk in range(8):
            k = 8 * c + kk
            a = flat[c, pl.ds(kk, 128, stride=8), :].T
            at[k] = a
            ax = ax + a * xs[pl.ds(k, 1), :]
            ab = ab + a * bs[pl.ds(k, 1), :]
        return ax, ab

    def later(i, held):
        ax, ab = held
        for kk in range(8):
            k = 8 * i + kk
            a = at[k]
            ax = ax + a * xs[pl.ds(k, 1), :]
            ab = ab + a * bs[pl.ds(k, 1), :]
        return ax, ab

    def product(step):
        ax, ab = lax.fori_loop(0, 16, later if step else first, (zero, zero))
        xs[...] = ax
        if step + 1 < STEPS:
            bs[...] = ab
            xb[step + 1] = ab
            free_m.append(rows_sum(ax * go[...]))
            gain_m.append(rows_sum(ab * go[...]))

    def a_copy(b, k):
        return copy(asend.at[b, k], arecv.at[b, k], a_s.at[b, k], a_r.at[b, k], net(k), d)

    def send_batch(b, values):
        table = [value * seat for value in values]
        table.append(jnp.zeros((128 - CAP * len(values), 128), F32))
        packed = sum(nt(own, piece) for piece in parts(jnp.concatenate(table, axis=0)))
        asend[b, :, 0, :] = packed
        arecv[b, 0] = packed[0:1, :]
        others(lambda k: a_copy(b, k).start())

    def v_copy(b, j):
        return copy(vall.at[b, d], vall.at[b, d], v_s.at[b, j], v_r.at[b, d], n, dev(j))

    def v_wait(b, j):
        return copy(vall.at[b, dev(j)], vall.at[b, dev(j)], v_s.at[b, j], v_r.at[b, dev(j)], n, dev(j))

    def share_batch(b):
        others(lambda k: a_copy(b, k).wait_recv())
        mask = one(iota((CAP, 128), 1) % CAP == iota((CAP, 128), 0))
        collect = one(iota((8, 128), 1) // CAP == iota((8, 128), 0)).astype(BF16)
        spread = jnp.concatenate([arecv[b, k] * mask for k in range(NETS)], axis=0)
        vall[b, d] = sum(nt(collect, piece) for piece in parts(spread))
        for j in range(1, DEVS):
            v_copy(b, j).start()

    row = iota((8, 1), 0)
    row_high = ((row // 2) * 8 + 2 * d + row % 2).astype(F32)
    row32 = iota((32, 1), 0)
    high32 = (((row32 % 8) // 2) * 8 + 2 * (row32 // 8) + row32 % 2).astype(F32)
    slot_high = []

    def place_batch(b, count):
        total = jnp.zeros((24 * count, 128), F32)
        for j in range(DEVS):
            if j:
                v_wait(b, j).wait_recv()
            vals = vall[b, dev(j)]
            if b == 0:
                bus = vals[3:4, :] - 1.0
                b_high = jnp.floor(bus * (1.0 / 128.0))
                slot_high.append(b_high)
                hots[j] = one(iota_f((128, 512), 0) == bus - 128.0 * b_high).astype(BF16)
                brow[j] = one(b_high == row_high)
            held = brow[j]
            left = jnp.concatenate([vals[q:q + 1, :] * held for q in range(count)], axis=0)
            total = total + nt(jnp.concatenate(parts(left), axis=0), hots[j])
        total = third_sum(total)
        return [total[8 * q:8 * q + 8] for q in range(count)]

    product(0)
    pl.semaphore_wait(bar, NETS - 1 + 3 * (DEVS - 1))
    line_copy = copy(pack, prev, l_s, l_r, net(1), d)
    line_copy.start()
    send_batch(0, [free_m[0], free_m[1], gain_m[0], bus_v[...].astype(F32) + 1.0])
    product(1)
    product(2)
    product(3)
    send_batch(1, free_m[2:5] + gain_m[1:4])

    line_copy.wait_recv()
    ends = jnp.concatenate([from_v[...].astype(F32), prev[0:1, :]], axis=1)
    delay = jnp.concatenate([pack[1:2, :], prev[1:2, :]], axis=1)
    twice = 2.0 / jnp.concatenate([pack[2:3, :], prev[2:3, :]], axis=1)
    waves = [jnp.concatenate([tp[i:i + 1, :], prev[3 + i:4 + i, :]], axis=1) for i in range(DMAX)]
    high = jnp.floor(ends * (1.0 / 128.0))
    ohl[...] = one(iota_f((128, 1024), 0) == ends - 128.0 * high).astype(BF16)
    mine = rows_sum(one(high == row_high))

    def arrivals(t):
        got = jnp.zeros((1, 1024), F32)
        for lag in range(DMIN, DMAX + 1):
            if DMAX + t - lag < len(waves):
                got = jnp.where(delay == float(lag), waves[DMAX + t - lag], got)
        return got

    def inject(t):
        left = jnp.concatenate(parts(one(high == high32) * arrive[t]), axis=0)
        jl[t] = third_sum(nt(left, ohl[...])).reshape(DEVS, 8, 128)

    def sample(v):
        left = jnp.concatenate(parts(v), axis=0)
        return rows_sum(third_sum(nn(left, ohl[...])) * one(high == row_high))

    arrive = [arrivals(0), arrivals(1)]
    inject(0)
    inject(1)

    def uv_copy(t, j):
        return copy(uv.at[t, d], uv.at[t, d], uv_s.at[t, j], uv_r.at[t, d], n, dev(j))

    def uv_wait(t, j):
        return copy(uv.at[t, dev(j)], uv.at[t, dev(j)], uv_s.at[t, j], uv_r.at[t, dev(j)], n, dev(j))

    def uv_send(t, u, v):
        uv[t, d, 0] = u
        uv[t, d, 1] = v
        for j in (2, 1, 3):
            uv_copy(t, j).start()

    def w_copy(t, way, j):
        return copy(wsend.at[t, way], wrecv.at[t, way, d], w_s.at[t, way, j], w_r.at[t, way, d],
                    net(1 if way == 0 else NETS - 1), dev(j))

    def w_wait(t, way, j):
        return copy(wsend.at[t, way], wrecv.at[t, way, dev(j)], w_s.at[t, way, j], w_r.at[t, way, dev(j)],
                    net(1 if way == 0 else NETS - 1), dev(j))

    def send_waves(t):
        wave = mine * (sample(volts[t]) * twice - arrive[t])
        wsend[t, 0] = wave[:, :512]
        wsend[t, 1] = wave[:, 512:]
        for j in (2, 1, 3, 0):
            for way in range(2):
                w_copy(t, way, j).start()

    def take_waves(t):
        for way in range(2):
            for j in range(DEVS):
                w_wait(t, way, j).wait_recv()
        waves.append(jnp.concatenate([sum(wrecv[t, 1, j] for j in range(DEVS)),
                                      sum(wrecv[t, 0, j] for j in range(DEVS))], axis=1))
        arrive.append(arrivals(t + DMIN))
        inject(t + DMIN)

    def columns(t, c, s):
        tiles = uv[t, c, 0] + jl[t, c]
        total = None
        for e in range(2):
            lanes = pl.ds(pl.multiple_of(256 * c + 128 * e, 128), 128)
            term = z[s, :, lanes] * tiles[2 * s + e:2 * s + e + 1, :]
            total = term if total is None else total + term
        return total

    def solve(t):
        uv_wait(t, 1).wait_recv()
        uv_wait(t, 3).wait_recv()
        for s in range(4):
            acc[s] = columns(t, d, s) + columns(t, dev(1), s) + columns(t, dev(3), s)
        uv_wait(t, 2).wait_recv()
        rows = []
        for s in range(4):
            total = acc[s] + columns(t, dev(2), s)
            rows.append(rows_sum(total[:128].T))
            rows.append(rows_sum(total[128:].T))
        return jnp.concatenate(rows, axis=0)

    def keep(t):
        for c in range(8):
            for s in range(4):
                spot = 1024 * s + 128 * c
                trace[t:t + 1, spot:spot + 128] = uv[t + 1, c // 2, 1, 2 * s + c % 2:2 * s + c % 2 + 1, :]

    def r_copy(b, k):
        return copy(rsend.at[b, k], rrecv.at[b, k], r_s.at[b, k], r_r.at[b, k], net(NETS - k), d)

    def send_back(b, steps):
        full = jnp.concatenate([uv[t + 1, c, 1] for t in steps for c in range(DEVS)], axis=0)
        reached = sum(nn(piece, hots[0]) for piece in parts(full))
        pick = one(slot_high[0] == high32)
        seats = one(iota((CAP, 512), 1) % CAP == iota((CAP, 512), 0))
        home = one(iota((NETS, 512), 1) // CAP == iota((NETS, 512), 0)).astype(BF16)
        table = [rows_sum(reached[32 * i:32 * i + 32] * pick) * seats for i in range(len(steps))]
        table.append(jnp.zeros((128 - CAP * len(steps), 512), F32))
        back = sum(nt(home, piece) for piece in parts(jnp.concatenate(table, axis=0)))
        rsend[b, :, 0, :] = back
        rrecv[b, 0] = back[0:1, :]
        others(lambda k: r_copy(b, k).start())

    def add_back(b, steps, state):
        others(lambda k: r_copy(b, k).wait_recv())
        answer = rrecv[b, :, 0, :]
        at_model = sum(tn(piece, own) for piece in parts(answer))
        for i, t in enumerate(steps):
            state = state + rows_sum(at_model[CAP * i:CAP * i + CAP] * seat) * xb[STEPS - 1 - t]
        return state

    share_batch(0)
    product(4)
    product(5)
    free, gain, volts = [], [], []
    got = place_batch(0, 3)
    free += got[:2]
    gain += got[2:]
    for load in loads[11:]:
        load.wait()
    base = jnp.concatenate([src[s, d] for s in range(4)], axis=0)
    uv_send(0, base + free[0], jnp.zeros((8, 128), F32))
    for t in range(STEPS):
        if t == 0:
            product(6)
            send_batch(2, free_m[5:8] + gain_m[4:7])
            share_batch(1)
        if 1 <= t <= STEPS - DMIN:
            send_waves(t - 1)
        if t == 1:
            got = place_batch(1, 6)
            free += got[:3]
            gain += got[3:]
        if t == 2:
            share_batch(2)
        if t >= 2:
            take_waves(t - 2)
            keep(t - 2)
        if t == 3:
            got = place_batch(2, 6)
            free += got[:3]
            gain += got[3:]
        if t == 4:
            product(7)
        ready = base
        if t + 1 < STEPS:
            ready = ready + free[t + 1]
            for k in range(t):
                ready = ready + gain[t - k] * volts[k]
        v = solve(t)
        volts.append(v)
        uv_send(t + 1, ready + gain[0] * v if t + 1 < STEPS else jnp.zeros((8, 128), F32), v)
    keep(STEPS - 2)
    send_back(0, list(range(STEPS - 1)))
    for j in range(1, DEVS):
        uv_wait(STEPS, j).wait_recv()
    send_back(1, [STEPS - 1])
    keep(STEPS - 1)

    def drain(k):
        for b in range(3):
            a_copy(b, k).wait_send()

    others(drain)
    line_copy.wait_send()
    for j in range(1, DEVS):
        for b in range(3):
            v_copy(b, j).wait_send()
        for t in range(STEPS + 1):
            uv_copy(t, j).wait_send()
    for t in range(STEPS - DMIN):
        for way in range(2):
            for j in range(DEVS):
                w_copy(t, way, j).wait_send()
    state = add_back(0, list(range(STEPS - 1)), xs[...])
    state = add_back(1, [STEPS - 1], state)
    final[...] = state.T

    def drain_back(k):
        for b in range(2):
            r_copy(b, k).wait_send()

    others(drain_back)


def body(zinv, source, model_state, propagator, input_gain, output_gain, model_owner, model_bus,
         line_from, line_to, line_delay, line_imped, wave_from_past, wave_to_past):
    vmem, dma = pltpu.VMEM, pltpu.SemaphoreType.DMA
    i32 = jnp.int32
    scratch = [
        vmem((4, 256, 1024), F32), vmem((4, DEVS, 2, 128), F32), vmem((128, 128), F32), vmem((128, 128), F32),
        vmem((128, 128), F32), vmem((1, 128), i32), vmem((1, 128), i32), vmem((1, 512), i32), vmem((1, 512), i32),
        vmem((1, 512), i32), vmem((1, 512), F32), vmem((DMAX, 512), F32), vmem((DMAX, 512), F32),
        vmem((16, 128, 8, 128), F32), vmem((128, 128, 128), F32), vmem((128, 128), F32), vmem((128, 128), F32),
        vmem((STEPS, 128, 128), F32), vmem((3, NETS, 1, 128), F32), vmem((3, NETS, 1, 128), F32),
        vmem((3, DEVS, 8, 512), F32), vmem((STEPS + 1, DEVS, 2, 8, 128), F32), vmem((16, 512), F32),
        vmem((16, 512), F32), vmem((6, 2, 1, 512), F32), vmem((6, 2, DEVS, 1, 512), F32),
        vmem((2, NETS, 1, 128), F32), vmem((2, NETS, 1, 128), F32), vmem((128, 1024), BF16),
        vmem((DEVS, 128, 512), BF16), vmem((DEVS, 8, 512), F32), vmem((4, 256, 128), F32),
        vmem((STEPS, DEVS, 8, 128), F32),
        dma((13,)), dma((16,)), dma((3, NETS)), dma((3, NETS)), dma((3, DEVS)), dma((3, DEVS)),
        dma((STEPS + 1, DEVS)), dma((STEPS + 1, DEVS)), dma((6, 2, DEVS)), dma((6, 2, DEVS)), dma, dma,
        dma((2, NETS)), dma((2, NETS)),
    ]
    v = pl.BlockSpec(memory_space=vmem)
    return pl.pallas_call(
        grid_kernel,
        out_shape=(jax.ShapeDtypeStruct((STEPS, 4096), F32), jax.ShapeDtypeStruct((128, 128), F32)),
        in_specs=[pl.BlockSpec(memory_space=pl.ANY)] * 14,
        out_specs=(v, v),
        scratch_shapes=scratch,
        compiler_params=pltpu.CompilerParams(collective_id=0, has_side_effects=True, vmem_limit_bytes=56 << 20),
    )(zinv, source.reshape(4, DEVS, 2, 128), model_state, propagator, input_gain, output_gain,
      model_owner.reshape(1, 128), model_bus.reshape(1, 128), line_from.reshape(1, 512), line_to.reshape(1, 512),
      line_delay.reshape(1, 512), line_imped.reshape(1, 512), wave_from_past, wave_to_past)


def solution(mesh):
    one_axis, both = P("net"), P(("net", "dev"))
    two = P(("net", "dev"), None)
    in_specs = (P("net", "dev", None), one_axis, two, P(("net", "dev"), None, None), two, two, two, both,
                one_axis, one_axis, one_axis, one_axis, P(None, "net"), P(None, "net"))
    return jax.shard_map(body, mesh=mesh, in_specs=in_specs, out_specs=(P(None, "net"), two), check_vma=False)
```

time: 101 us -> 73.5 us (0.73)
  Pallas kernels: 86.4 us -> 69.7 us
  local copies, waits for them, and re-layouts: 9.52 us -> 3.04 us
  other arithmetic: 3.44 us -> 0 us
    pallas_call x2 -> x1, Pallas kernels: 86.4 us -> 69.7 us  [body(): pl.pallas_call(grid_kernel, out_shape=(jax.ShapeDtypeStruct((STEPS, 4096)...]
    unnamed x14 -> x2, local copies, waits for them, and re-layouts: 7.19 us -> 3.04 us
    convert_element_type x4 -> x0, other arithmetic: 2.71 us -> none  [r(): return x.astype(F32)[None, :]]
    concatenate x2 -> x0, local copies, waits for them, and re-layouts: 2.33 us -> none  [the longest x1 2.25 us: body(): jnp.concatenate([r(line_to), r(line_delay), r(line_imped), wave_from_past...]
where the time goes in v2:
time: 73.5 us; the launch traced here: 73.4 us
  Pallas kernels  69.7 us (95%)
  local copies, waits for them, and re-layouts  3.04 us (4%)
    pallas_call x1, Pallas kernels, body(): pl.pallas_call(grid_kernel, out_shape=(jax.ShapeDtypeStruct((STEPS, 4096)...  69.7 us
    unnamed x2, local copies, waits for them, and re-layouts  3.04 us

profile of v2, /device:TPU:1, one launch (start us, length us, event | category | flops | bytes accessed | tf_op | source)
XLA Modules:
  0.0 73.4 jit_solution(16767955847939030786)
XLA Ops:
  0.6 69.7 %shard_map.149 = (f32[8,4096]{1,0:T(8,128)}, f32[128,128]{1,0:T(8,128)}) custom-call(f32[4,256,1024]{2,1,0:T(8,128)} %zinv.1, f32[4,4,2,128]{3,2,1,0:T(2,128)} %bitcast.7, f32[128,128]{1,0:T(8,128)} %state0.1, f32[128,128,128]{2,1,0:T(8,128)} %prop.1, f32[128,128]{1,0:T(8,128)} %bgain.1, f32[128,128]{1,0:T(8,128)} %ogain.1, s32[1,128]{1,0:T(1,128)} %bitcast.12, ...), custom_call_target="tpu_custom_call" | custom-call | tf_op jit(solution)/shard_map/pallas_call | solution.py:441
  70.3 1.6 %copy.18 = f32[8,4096]{1,0:T(8,128)} copy(f32[8,4096]{1,0:T(8,128)} %get-tuple-element.4) | data formatting | bytes 262144
  71.9 1.5 %copy.19 = f32[128,128]{1,0:T(8,128)} copy(f32[128,128]{1,0:T(8,128)} %get-tuple-element.5) | data formatting | bytes 131072

commit v3 on v2

--- a/solution.py
+++ b/solution.py
@@ -63,6 +63,9 @@
     return x[:rows] + x[rows:2 * rows] + x[2 * rows:]
 
 
+FAR_FIRST = sorted(range(1, NETS), key=lambda k: -min(k // 8, 4 - k // 8) - min(k // 2 % 4, 4 - k // 2 % 4) - k % 2)
+
+
 def grid_kernel(zinv, source, state0, prop, bgain, ogain, owner_i, bus_i, from_i, to_i, delay_i, imped_i, fpast, tpast,
                 trace, final,
                 z, src, st, gi, go, own_v, bus_v, from_v, to_v, delay_v, imped_v, fp, tp,
@@ -72,8 +75,16 @@
     n = lax.axis_index("net")
     d = lax.axis_index("dev")
 
+    x = n // 8
+    y = (n // 2) % 4
+    core = n % 2
+
     def net(k):
         return lax.rem(n + k, NETS)
+
+    def away(k, way=1):
+        kx, ky, kc = way * (k // 8) + 4, way * ((k // 2) % 4) + 4, k % 2
+        return lax.rem(x + kx, 4) * 8 + lax.rem(y + ky, 4) * 2 + lax.rem(core + kc, 2)
 
     def dev(j):
         return lax.rem(d + j, DEVS)
@@ -81,9 +92,6 @@
     def copy(a, b, send, recv, to_net, to_dev):
         return pltpu.make_async_remote_copy(src_ref=a, dst_ref=b, send_sem=send, recv_sem=recv,
                                             device_id=(to_net, to_dev), device_id_type=MESH)
-
-    def others(run):
-        lax.fori_loop(1, NETS, lambda k, _: (run(k), 0)[1], 0)
 
     pairs = [(state0, st), (bgain, gi), (ogain, go), (owner_i, own_v), (bus_i, bus_v), (from_i, from_v), (to_i, to_v),
              (delay_i, delay_v), (imped_i, imped_v), (fpast, fp), (tpast, tp), (source, src), (zinv, z)]
@@ -104,7 +112,7 @@
     def greet(to_net, to_dev):
         pl.semaphore_signal(bar, inc=1, device_id=(to_net, to_dev), device_id_type=MESH)
 
-    others(lambda k: greet(net(k), d))
+    lax.fori_loop(1, NETS, lambda k, _: (greet(net(k), d), 0)[1], 0)
     for j in range(1, DEVS):
         greet(n, dev(j))
         greet(net(1), dev(j))
@@ -113,8 +121,15 @@
     for load in loads[:11]:
         load.wait()
     owner = own_v[...].astype(F32)
-    offset = owner - n.astype(F32)
-    offset = jnp.where(offset < 0.0, offset + float(NETS), offset)
+    own_x = jnp.floor(owner * 0.125)
+    own_y = jnp.floor((owner - 8.0 * own_x) * 0.5)
+    own_c = owner - 8.0 * own_x - 2.0 * own_y
+
+    def steps_to(to, at, size):
+        gap = to - at.astype(F32)
+        return jnp.where(gap < 0.0, gap + size, gap)
+
+    offset = 8.0 * steps_to(own_x, x, 4.0) + 2.0 * steps_to(own_y, y, 4.0) + steps_to(own_c, core, 2.0)
     wide = jnp.broadcast_to(owner, (128, 128))
     earlier = one(wide.T == wide) * one(iota((128, 128), 0) < iota((128, 128), 1))
     rank = rows_sum(earlier)
@@ -168,7 +183,11 @@
             gain_m.append(rows_sum(ab * go[...]))
 
     def a_copy(b, k):
-        return copy(asend.at[b, k], arecv.at[b, k], a_s.at[b, k], a_r.at[b, k], net(k), d)
+        return copy(asend.at[b, k], arecv.at[b, k], a_s.at[b], a_r.at[b], away(k), d)
+
+    def a_all(b):
+        rest = pl.ds(1, NETS - 1)
+        return copy(asend.at[b, rest], arecv.at[b, rest], a_s.at[b], a_r.at[b], away(1), d)
 
     def send_batch(b, values):
         table = [value * seat for value in values]
@@ -176,7 +195,8 @@
         packed = sum(nt(own, piece) for piece in parts(jnp.concatenate(table, axis=0)))
         asend[b, :, 0, :] = packed
         arecv[b, 0] = packed[0:1, :]
-        others(lambda k: a_copy(b, k).start())
+        for k in FAR_FIRST:
+            a_copy(b, k).start()
 
     def v_copy(b, j):
         return copy(vall.at[b, d], vall.at[b, d], v_s.at[b, j], v_r.at[b, d], n, dev(j))
@@ -185,7 +205,7 @@
         return copy(vall.at[b, dev(j)], vall.at[b, dev(j)], v_s.at[b, j], v_r.at[b, dev(j)], n, dev(j))
 
     def share_batch(b):
-        others(lambda k: a_copy(b, k).wait_recv())
+        a_all(b).wait_recv()
         mask = one(iota((CAP, 128), 1) % CAP == iota((CAP, 128), 0))
         collect = one(iota((8, 128), 1) // CAP == iota((8, 128), 0)).astype(BF16)
         spread = jnp.concatenate([arecv[b, k] * mask for k in range(NETS)], axis=0)
@@ -199,8 +219,10 @@
     high32 = (((row32 % 8) // 2) * 8 + 2 * (row32 // 8) + row32 % 2).astype(F32)
     slot_high = []
 
-    def place_batch(b, count):
-        total = jnp.zeros((24 * count, 128), F32)
+    def place_batch(b):
+        first_rows = 32 if b == 0 else 8
+        count = 3 if b == 0 else 4
+        total = jnp.zeros((3 * (first_rows + 8 * (count - 1)), 128), F32)
         for j in range(DEVS):
             if j:
                 v_wait(b, j).wait_recv()
@@ -212,10 +234,11 @@
                 hots[j] = one(iota_f((128, 512), 0) == bus - 128.0 * b_high).astype(BF16)
                 brow[j] = one(b_high == row_high)
             held = brow[j]
-            left = jnp.concatenate([vals[q:q + 1, :] * held for q in range(count)], axis=0)
+            whole = one(b_high == high32) if b == 0 else held
+            left = jnp.concatenate([vals[0:1, :] * whole] + [vals[q:q + 1, :] * held for q in range(1, count)], axis=0)
             total = total + nt(jnp.concatenate(parts(left), axis=0), hots[j])
         total = third_sum(total)
-        return [total[8 * q:8 * q + 8] for q in range(count)]
+        return [total[:first_rows]] + [total[first_rows + 8 * q:first_rows + 8 * q + 8] for q in range(count - 1)]
 
     product(0)
     pl.semaphore_wait(bar, NETS - 1 + 3 * (DEVS - 1))
@@ -224,8 +247,8 @@
     send_batch(0, [free_m[0], free_m[1], gain_m[0], bus_v[...].astype(F32) + 1.0])
     product(1)
     product(2)
-    product(3)
-    send_batch(1, free_m[2:5] + gain_m[1:4])
+    send_batch(1, free_m[2:4] + gain_m[1:3])
+    share_batch(0)
 
     line_copy.wait_recv()
     ends = jnp.concatenate([from_v[...].astype(F32), prev[0:1, :]], axis=1)
@@ -256,10 +279,14 @@
     inject(1)
 
     def uv_copy(t, j):
-        return copy(uv.at[t, d], uv.at[t, d], uv_s.at[t, j], uv_r.at[t, d], n, dev(j))
+        return copy(uv.at[t, d], uv.at[t, d], uv_s.at[t], uv_r.at[t, d], n, dev(j))
 
     def uv_wait(t, j):
-        return copy(uv.at[t, dev(j)], uv.at[t, dev(j)], uv_s.at[t, j], uv_r.at[t, dev(j)], n, dev(j))
+        return copy(uv.at[t, dev(j)], uv.at[t, dev(j)], uv_s.at[t], uv_r.at[t, dev(j)], n, dev(j))
+
+    def uv_all(t):
+        sent = uv.at[t, pl.ds(0, DEVS - 1)]
+        return copy(sent, sent, uv_s.at[t], uv_r.at[t, d], n, dev(1))
 
     def uv_send(t, u, v):
         uv[t, d, 0] = u
@@ -268,12 +295,10 @@
             uv_copy(t, j).start()
 
     def w_copy(t, way, j):
-        return copy(wsend.at[t, way], wrecv.at[t, way, d], w_s.at[t, way, j], w_r.at[t, way, d],
-                    net(1 if way == 0 else NETS - 1), dev(j))
-
-    def w_wait(t, way, j):
-        return copy(wsend.at[t, way], wrecv.at[t, way, dev(j)], w_s.at[t, way, j], w_r.at[t, way, dev(j)],
-                    net(1 if way == 0 else NETS - 1), dev(j))
+        return copy(wsend.at[t, way], wrecv.at[t, way, d], w_s.at[t], w_r.at[t], net(1 if way == 0 else NETS - 1), dev(j))
+
+    def w_all(t):
+        return copy(wrecv.at[t], wrecv.at[t], w_s.at[t], w_r.at[t], net(1), d)
 
     def send_waves(t):
         wave = mine * (sample(volts[t]) * twice - arrive[t])
@@ -284,9 +309,7 @@
                 w_copy(t, way, j).start()
 
     def take_waves(t):
-        for way in range(2):
-            for j in range(DEVS):
-                w_wait(t, way, j).wait_recv()
+        w_all(t).wait_recv()
         waves.append(jnp.concatenate([sum(wrecv[t, 1, j] for j in range(DEVS)),
                                       sum(wrecv[t, 0, j] for j in range(DEVS))], axis=1))
         arrive.append(arrivals(t + DMIN))
@@ -302,11 +325,13 @@
         return total
 
     def solve(t):
-        uv_wait(t, 1).wait_recv()
-        uv_wait(t, 3).wait_recv()
+        if t:
+            uv_wait(t, 1).wait_recv()
+            uv_wait(t, 3).wait_recv()
         for s in range(4):
             acc[s] = columns(t, d, s) + columns(t, dev(1), s) + columns(t, dev(3), s)
-        uv_wait(t, 2).wait_recv()
+        if t:
+            uv_wait(t, 2).wait_recv()
         rows = []
         for s in range(4):
             total = acc[s] + columns(t, dev(2), s)
@@ -321,7 +346,11 @@
                 trace[t:t + 1, spot:spot + 128] = uv[t + 1, c // 2, 1, 2 * s + c % 2:2 * s + c % 2 + 1, :]
 
     def r_copy(b, k):
-        return copy(rsend.at[b, k], rrecv.at[b, k], r_s.at[b, k], r_r.at[b, k], net(NETS - k), d)
+        return copy(rsend.at[b, k], rrecv.at[b, k], r_s.at[b], r_r.at[b], away(k, -1), d)
+
+    def r_all(b):
+        rest = pl.ds(1, NETS - 1)
+        return copy(rsend.at[b, rest], rrecv.at[b, rest], r_s.at[b], r_r.at[b], away(1), d)
 
     def send_back(b, steps):
         full = jnp.concatenate([uv[t + 1, c, 1] for t in steps for c in range(DEVS)], axis=0)
@@ -334,49 +363,51 @@
         back = sum(nt(home, piece) for piece in parts(jnp.concatenate(table, axis=0)))
         rsend[b, :, 0, :] = back
         rrecv[b, 0] = back[0:1, :]
-        others(lambda k: r_copy(b, k).start())
-
-    def add_back(b, steps, state):
-        others(lambda k: r_copy(b, k).wait_recv())
-        answer = rrecv[b, :, 0, :]
-        at_model = sum(tn(piece, own) for piece in parts(answer))
-        for i, t in enumerate(steps):
-            state = state + rows_sum(at_model[CAP * i:CAP * i + CAP] * seat) * xb[STEPS - 1 - t]
-        return state
-
-    share_batch(0)
+        for k in FAR_FIRST:
+            r_copy(b, k).start()
+
+    def at_models(b):
+        r_all(b).wait_recv()
+        return parts(rrecv[b, :, 0, :])
+
+    product(3)
     product(4)
-    product(5)
     free, gain, volts = [], [], []
-    got = place_batch(0, 3)
+    got = place_batch(0)
     free += got[:2]
     gain += got[2:]
     for load in loads[11:]:
         load.wait()
+    for c in range(DEVS):
+        uv[0, c, 0] = jnp.concatenate([src[s, c] for s in range(4)], axis=0) + free[0][8 * c:8 * c + 8]
     base = jnp.concatenate([src[s, d] for s in range(4)], axis=0)
-    uv_send(0, base + free[0], jnp.zeros((8, 128), F32))
     for t in range(STEPS):
-        if t == 0:
-            product(6)
-            send_batch(2, free_m[5:8] + gain_m[4:7])
+        if t == 1:
             share_batch(1)
         if 1 <= t <= STEPS - DMIN:
             send_waves(t - 1)
         if t == 1:
-            got = place_batch(1, 6)
-            free += got[:3]
-            gain += got[3:]
+            send_batch(2, free_m[4:6] + gain_m[3:5])
+        if t == 2:
+            product(5)
+        if t == 3:
+            product(6)
+            send_batch(3, free_m[6:8] + gain_m[5:7])
+        if t == 4:
+            product(7)
+        if t >= 2:
+            take_waves(t - 2)
         if t == 2:
             share_batch(2)
-        if t >= 2:
-            take_waves(t - 2)
-            keep(t - 2)
-        if t == 3:
-            got = place_batch(2, 6)
-            free += got[:3]
-            gain += got[3:]
         if t == 4:
-            product(7)
+            share_batch(3)
+        if t % 2:
+            got = place_batch((t + 1) // 2) if t < 7 else []
+            free += got[:2]
+            gain += got[2:]
+        if t >= 5:
+            for old in ((0, 1), (2, 3), (4, 5))[t - 5]:
+                keep(old)
         ready = base
         if t + 1 < STEPS:
             ready = ready + free[t + 1]
@@ -385,37 +416,32 @@
         v = solve(t)
         volts.append(v)
         uv_send(t + 1, ready + gain[0] * v if t + 1 < STEPS else jnp.zeros((8, 128), F32), v)
-    keep(STEPS - 2)
     send_back(0, list(range(STEPS - 1)))
     for j in range(1, DEVS):
         uv_wait(STEPS, j).wait_recv()
     send_back(1, [STEPS - 1])
+
+    keep(STEPS - 2)
     keep(STEPS - 1)
-
-    def drain(k):
-        for b in range(3):
-            a_copy(b, k).wait_send()
-
-    others(drain)
     line_copy.wait_send()
-    for j in range(1, DEVS):
-        for b in range(3):
+    for b in range(4):
+        a_all(b).wait_send()
+        for j in range(1, DEVS):
             v_copy(b, j).wait_send()
-        for t in range(STEPS + 1):
-            uv_copy(t, j).wait_send()
+    for t in range(1, STEPS + 1):
+        uv_all(t).wait_send()
     for t in range(STEPS - DMIN):
-        for way in range(2):
-            for j in range(DEVS):
-                w_copy(t, way, j).wait_send()
-    state = add_back(0, list(range(STEPS - 1)), xs[...])
-    state = add_back(1, [STEPS - 1], state)
-    final[...] = state.T
-
-    def drain_back(k):
-        for b in range(2):
-            r_copy(b, k).wait_send()
-
-    others(drain_back)
+        w_all(t).wait_send()
+    state = xs[...]
+    by_seat = sum(tn(piece, own) for piece in at_models(0))
+    for t in range(STEPS - 1):
+        state = state + rows_sum(by_seat[CAP * t:CAP * t + CAP] * seat) * xb[STEPS - 1 - t]
+    state = state.T
+    seat_cols = jnp.concatenate([seat, jnp.zeros((128 - CAP, 128), F32)], axis=0).T
+    for b in range(2):
+        r_all(b).wait_send()
+    by_model = sum(tn(own, piece) for piece in at_models(1))
+    final[...] = state + jnp.sum(by_model * seat_cols, axis=1, keepdims=True) * gi[...]
 
 
 def body(zinv, source, model_state, propagator, input_gain, output_gain, model_owner, model_bus,
@@ -427,20 +453,19 @@
         vmem((128, 128), F32), vmem((1, 128), i32), vmem((1, 128), i32), vmem((1, 512), i32), vmem((1, 512), i32),
         vmem((1, 512), i32), vmem((1, 512), F32), vmem((DMAX, 512), F32), vmem((DMAX, 512), F32),
         vmem((16, 128, 8, 128), F32), vmem((128, 128, 128), F32), vmem((128, 128), F32), vmem((128, 128), F32),
-        vmem((STEPS, 128, 128), F32), vmem((3, NETS, 1, 128), F32), vmem((3, NETS, 1, 128), F32),
-        vmem((3, DEVS, 8, 512), F32), vmem((STEPS + 1, DEVS, 2, 8, 128), F32), vmem((16, 512), F32),
+        vmem((STEPS, 128, 128), F32), vmem((4, NETS, 1, 128), F32), vmem((4, NETS, 1, 128), F32),
+        vmem((4, DEVS, 8, 512), F32), vmem((STEPS + 1, DEVS, 2, 8, 128), F32), vmem((16, 512), F32),
         vmem((16, 512), F32), vmem((6, 2, 1, 512), F32), vmem((6, 2, DEVS, 1, 512), F32),
         vmem((2, NETS, 1, 128), F32), vmem((2, NETS, 1, 128), F32), vmem((128, 1024), BF16),
         vmem((DEVS, 128, 512), BF16), vmem((DEVS, 8, 512), F32), vmem((4, 256, 128), F32),
         vmem((STEPS, DEVS, 8, 128), F32),
-        dma((13,)), dma((16,)), dma((3, NETS)), dma((3, NETS)), dma((3, DEVS)), dma((3, DEVS)),
-        dma((STEPS + 1, DEVS)), dma((STEPS + 1, DEVS)), dma((6, 2, DEVS)), dma((6, 2, DEVS)), dma, dma,
-        dma((2, NETS)), dma((2, NETS)),
+        dma((13,)), dma((16,)), dma((4,)), dma((4,)), dma((4, DEVS)), dma((4, DEVS)),
+        dma((STEPS + 1,)), dma((STEPS + 1, DEVS)), dma((6,)), dma((6,)), dma, dma, dma((2,)), dma((2,)),
     ]
     v = pl.BlockSpec(memory_space=vmem)
     return pl.pallas_call(
         grid_kernel,
-        out_shape=(jax.ShapeDtypeStruct((STEPS, 4096), F32), jax.ShapeDtypeStruct((128, 128), F32)),
+        out_shape=(vmem((STEPS, 4096), F32), vmem((128, 128), F32)),
         in_specs=[pl.BlockSpec(memory_space=pl.ANY)] * 14,
         out_specs=(v, v),
         scratch_shapes=scratch,

time: 73.5 us -> 62.1 us (0.84)
  Pallas kernels: 69.7 us -> 60.1 us
  local copies, waits for them, and re-layouts: 3.04 us -> 1.29 us
    pallas_call x1, Pallas kernels: 69.7 us -> 60.1 us  [body(): pl.pallas_call(grid_kernel, out_shape=(vmem((STEPS, 4096), F32), vmem((12...]
    unnamed x2, local copies, waits for them, and re-layouts: 3.04 us -> 1.29 us
where the time goes in v3:
time: 62.1 us; the launch traced here: 62 us
  Pallas kernels  60.1 us (97%)
  local copies, waits for them, and re-layouts  1.29 us (2%)
  between operations  0.64 us (1%)
    pallas_call x1, Pallas kernels, body(): pl.pallas_call(grid_kernel, out_shape=(vmem((STEPS, 4096), F32), vmem((12...  60.1 us
    unnamed x2, local copies, waits for them, and re-layouts  1.29 us

profile of v3, /device:TPU:1, one launch (start us, length us, event | category | flops | bytes accessed | tf_op | source)
XLA Modules:
  0.0 62.0 jit_solution(7797626513558783108)
XLA Ops:
  0.6 60.1 %shard_map.149 = (f32[8,4096]{1,0:T(8,128)S(1)}, f32[128,128]{1,0:T(8,128)S(1)}) custom-call(f32[4,256,1024]{2,1,0:T(8,128)} %zinv.1, f32[4,4,2,128]{3,2,1,0:T(2,128)} %bitcast.7, f32[128,128]{1,0:T(8,128)} %state0.1, f32[128,128,128]{2,1,0:T(8,128)} %prop.1, f32[128,128]{1,0:T(8,128)} %bgain.1, f32[128,128]{1,0:T(8,128)} %ogain.1, s32[1,128]{1,0:T(1,128)} %bitcast.12, ...), custom_call_target="tpu_custom_call" | custom-call | tf_op jit(solution)/shard_map/pallas_call | solution.py:466
  60.7 0.7 %copy.18 = f32[8,4096]{1,0:T(8,128)} copy(f32[8,4096]{1,0:T(8,128)S(1)} %get-tuple-element.2) | data formatting | bytes 262144
  61.4 0.6 %copy.19 = f32[128,128]{1,0:T(8,128)} copy(f32[128,128]{1,0:T(8,128)S(1)} %get-tuple-element.3) | data formatting | bytes 131072

commit v4 on v3

--- a/solution.py
+++ b/solution.py
@@ -11,6 +11,7 @@
 NETS = 32
 DEVS = 4
 CAP = 16
+PARTS = 2
 F32 = jnp.float32
 BF16 = jnp.bfloat16
 MESH = pl.DeviceIdType.MESH
@@ -20,7 +21,7 @@
     return jnp.sum(x, axis=0, keepdims=True)
 
 
-def parts(x, count=3):
+def parts(x, count=PARTS):
     pieces = []
     for i in range(count):
         piece = x.astype(BF16)
@@ -58,20 +59,26 @@
     return jnp.where(mask, 1.0, 0.0).astype(F32)
 
 
-def third_sum(x):
-    rows = x.shape[0] // 3
-    return x[:rows] + x[rows:2 * rows] + x[2 * rows:]
-
-
-FAR_FIRST = sorted(range(1, NETS), key=lambda k: -min(k // 8, 4 - k // 8) - min(k // 2 % 4, 4 - k // 2 % 4) - k % 2)
+def add_parts(x):
+    rows = x.shape[0] // PARTS
+    return sum(x[rows * i:rows * i + rows] for i in range(PARTS))
+
+
+def hops(k):
+    x, y, z = (min(v, 4 - v) for v in (k // 8 % 4, k // 2 % 4, k // 32))
+    return x + y + z + k % 2 * 0.5
+
+
+FAR_FIRST = sorted(range(1, NETS), key=hops, reverse=True)
+ALL_FAR_FIRST = sorted(range(1, NETS * DEVS), key=hops, reverse=True)
 
 
 def grid_kernel(zinv, source, state0, prop, bgain, ogain, owner_i, bus_i, from_i, to_i, delay_i, imped_i, fpast, tpast,
                 trace, final,
                 z, src, st, gi, go, own_v, bus_v, from_v, to_v, delay_v, imped_v, fp, tp,
-                raw, at, xs, bs, xb, asend, arecv, vall, uv, pack, prev, wsend, wrecv, rsend, rrecv,
+                raw, at, xp, xb, rp, asend, arecv, arecv0, vall, uv, pack, prev, wsend, wrecv, rsend, rrecv, lsend, lrecv,
                 ohl, hots, brow, acc, jl,
-                in_s, raw_s, a_s, a_r, v_s, v_r, uv_s, uv_r, w_s, w_r, l_s, l_r, r_s, r_r):
+                in_s, raw_s, a_s, a_r, v_s, v_r, uv_s, uv_r, w_s, w_r, l_s, l_r, r_s, r_r, e_s, e_r):
     n = lax.axis_index("net")
     d = lax.axis_index("dev")
 
@@ -112,11 +119,14 @@
     def greet(to_net, to_dev):
         pl.semaphore_signal(bar, inc=1, device_id=(to_net, to_dev), device_id_type=MESH)
 
-    lax.fori_loop(1, NETS, lambda k, _: (greet(net(k), d), 0)[1], 0)
+    def greet_all(k, _):
+        for j in range(DEVS):
+            greet(net(k), dev(j))
+        return 0
+
+    lax.fori_loop(1, NETS, greet_all, 0)
     for j in range(1, DEVS):
         greet(n, dev(j))
-        greet(net(1), dev(j))
-        greet(net(NETS - 1), dev(j))
 
     for load in loads[:11]:
         load.wait()
@@ -135,15 +145,9 @@
     rank = rows_sum(earlier)
     own = one(iota_f((NETS, 128), 0) == offset).astype(BF16)
     seat = one(iota_f((CAP, 128), 0) == rank)
-    ogt = go[...].T
-    go[...] = ogt
-    first_x = st[...].T
-    first_b = gi[...].T
-    xs[...] = first_x
-    bs[...] = first_b
-    xb[0] = first_b
-    free_m = [rows_sum(first_x * ogt)]
-    gain_m = [rows_sum(first_b * ogt)]
+    xp[0] = st[...].T
+    xb[0] = gi[...].T
+    rp[0] = go[...].T
     pack[0:1, :] = to_v[...].astype(F32)
     pack[1:2, :] = delay_v[...].astype(F32)
     pack[2:3, :] = imped_v[...]
@@ -153,34 +157,40 @@
     flat = raw.reshape(16, 1024, 128)
     zero = jnp.zeros((128, 128), F32)
 
-    def first(c, held):
-        raw_copy(c).wait()
-        ax, ab = held
-        for kk in range(8):
-            k = 8 * c + kk
-            a = flat[c, pl.ds(kk, 128, stride=8), :].T
-            at[k] = a
-            ax = ax + a * xs[pl.ds(k, 1), :]
-            ab = ab + a * bs[pl.ds(k, 1), :]
-        return ax, ab
-
-    def later(i, held):
-        ax, ab = held
-        for kk in range(8):
-            k = 8 * i + kk
-            a = at[k]
-            ax = ax + a * xs[pl.ds(k, 1), :]
-            ab = ab + a * bs[pl.ds(k, 1), :]
-        return ax, ab
-
-    def product(step):
-        ax, ab = lax.fori_loop(0, 16, later if step else first, (zero, zero))
-        xs[...] = ax
-        if step + 1 < STEPS:
-            bs[...] = ab
-            xb[step + 1] = ab
-            free_m.append(rows_sum(ax * go[...]))
-            gain_m.append(rows_sum(ab * go[...]))
+    def passes(i, x=None, b=None, r=None):
+        def group(c, held):
+            ax, ab = held
+            if not i:
+                raw_copy(c).wait()
+            rows = []
+            for kk in range(8):
+                k = 8 * c + kk
+                if i:
+                    a = at[k]
+                else:
+                    a = flat[c, pl.ds(kk, 128, stride=8), :].T
+                    at[k] = a
+                if x is not None:
+                    ax = ax + a * xp[x, pl.ds(k, 1), :]
+                if b is not None:
+                    ab = ab + a * xb[b, pl.ds(k, 1), :]
+                if r is not None:
+                    rows.append(rows_sum(a * rp[r]))
+            if r is not None:
+                rp[r + 1, pl.ds(8 * c, 8), :] = jnp.concatenate(rows, axis=0)
+            return ax, ab
+
+        ax, ab = lax.fori_loop(0, 16, group, (zero if x is not None else 0, zero if b is not None else 0))
+        if x is not None:
+            xp[x + 1] = ax
+        if b is not None:
+            xb[b + 1] = ab
+
+    def free_of(i, j):
+        return rows_sum(xp[i] * rp[j])
+
+    def gain_of(i, j):
+        return rows_sum(xb[i] * rp[j])
 
     def a_copy(b, k):
         return copy(asend.at[b, k], arecv.at[b, k], a_s.at[b], a_r.at[b], away(k), d)
@@ -189,14 +199,27 @@
         rest = pl.ds(1, NETS - 1)
         return copy(asend.at[b, rest], arecv.at[b, rest], a_s.at[b], a_r.at[b], away(1), d)
 
+    def first_copy(g):
+        return copy(asend.at[0, g % NETS], arecv0.at[g], a_s.at[0], a_r.at[0], away(g % NETS), dev(g // NETS))
+
+    def first_all():
+        rest = pl.ds(1, NETS * DEVS - 1)
+        return copy(arecv0.at[rest], arecv0.at[rest], a_s.at[0], a_r.at[0], away(1), d)
+
     def send_batch(b, values):
         table = [value * seat for value in values]
-        table.append(jnp.zeros((128 - CAP * len(values), 128), F32))
+        if len(values) < 8:
+            table.append(jnp.zeros((128 - CAP * len(values), 128), F32))
         packed = sum(nt(own, piece) for piece in parts(jnp.concatenate(table, axis=0)))
         asend[b, :, 0, :] = packed
-        arecv[b, 0] = packed[0:1, :]
-        for k in FAR_FIRST:
-            a_copy(b, k).start()
+        if b:
+            arecv[b, 0] = packed[0:1, :]
+            for k in FAR_FIRST:
+                a_copy(b, k).start()
+        else:
+            arecv0[0] = packed[0:1, :]
+            for g in ALL_FAR_FIRST:
+                first_copy(g).start()
 
     def v_copy(b, j):
         return copy(vall.at[b, d], vall.at[b, d], v_s.at[b, j], v_r.at[b, d], n, dev(j))
@@ -204,12 +227,15 @@
     def v_wait(b, j):
         return copy(vall.at[b, dev(j)], vall.at[b, dev(j)], v_s.at[b, j], v_r.at[b, dev(j)], n, dev(j))
 
+    def unpack(ref, at):
+        mask = one(iota((CAP, 128), 1) % CAP == iota((CAP, 128), 0))
+        collect = one(iota((8, 128), 1) // CAP == iota((8, 128), 0)).astype(BF16)
+        spread = jnp.concatenate([ref[at + k] * mask for k in range(NETS)], axis=0)
+        return sum(nt(collect, piece) for piece in parts(spread))
+
     def share_batch(b):
         a_all(b).wait_recv()
-        mask = one(iota((CAP, 128), 1) % CAP == iota((CAP, 128), 0))
-        collect = one(iota((8, 128), 1) // CAP == iota((8, 128), 0)).astype(BF16)
-        spread = jnp.concatenate([arecv[b, k] * mask for k in range(NETS)], axis=0)
-        vall[b, d] = sum(nt(collect, piece) for piece in parts(spread))
+        vall[b, d] = unpack(arecv.at[b], 0)
         for j in range(1, DEVS):
             v_copy(b, j).start()
 
@@ -219,36 +245,35 @@
     high32 = (((row32 % 8) // 2) * 8 + 2 * (row32 // 8) + row32 % 2).astype(F32)
     slot_high = []
 
-    def place_batch(b):
-        first_rows = 32 if b == 0 else 8
-        count = 3 if b == 0 else 4
-        total = jnp.zeros((3 * (first_rows + 8 * (count - 1)), 128), F32)
+    def place_batch(b, count):
+        first_rows = 8 if b else 32
+        total = 0.0
         for j in range(DEVS):
-            if j:
-                v_wait(b, j).wait_recv()
-            vals = vall[b, dev(j)]
-            if b == 0:
-                bus = vals[3:4, :] - 1.0
+            if b:
+                if j:
+                    v_wait(b, j).wait_recv()
+                vals = vall[b, dev(j)]
+                whole = brow[j]
+            else:
+                vals = unpack(arecv0, NETS * ((DEVS - j) % DEVS))
+                bus = vals[7:8, :] - 1.0
                 b_high = jnp.floor(bus * (1.0 / 128.0))
                 slot_high.append(b_high)
                 hots[j] = one(iota_f((128, 512), 0) == bus - 128.0 * b_high).astype(BF16)
                 brow[j] = one(b_high == row_high)
-            held = brow[j]
-            whole = one(b_high == high32) if b == 0 else held
-            left = jnp.concatenate([vals[0:1, :] * whole] + [vals[q:q + 1, :] * held for q in range(1, count)], axis=0)
+                whole = one(b_high == high32)
+            left = jnp.concatenate([vals[0:1, :] * whole] + [vals[q:q + 1, :] * brow[j] for q in range(1, count)], axis=0)
             total = total + nt(jnp.concatenate(parts(left), axis=0), hots[j])
-        total = third_sum(total)
+        total = add_parts(total)
         return [total[:first_rows]] + [total[first_rows + 8 * q:first_rows + 8 * q + 8] for q in range(count - 1)]
 
-    product(0)
-    pl.semaphore_wait(bar, NETS - 1 + 3 * (DEVS - 1))
+    passes(0, x=0, b=0, r=0)
+    passes(1, x=1)
+    pl.semaphore_wait(bar, NETS * DEVS - 1)
     line_copy = copy(pack, prev, l_s, l_r, net(1), d)
     line_copy.start()
-    send_batch(0, [free_m[0], free_m[1], gain_m[0], bus_v[...].astype(F32) + 1.0])
-    product(1)
-    product(2)
-    send_batch(1, free_m[2:4] + gain_m[1:3])
-    share_batch(0)
+    send_batch(0, [free_of(0, 0), free_of(1, 0), free_of(1, 1), free_of(2, 1),
+                   gain_of(0, 0), gain_of(1, 0), gain_of(1, 1), bus_v[...].astype(F32) + 1.0])
 
     line_copy.wait_recv()
     ends = jnp.concatenate([from_v[...].astype(F32), prev[0:1, :]], axis=1)
@@ -268,11 +293,11 @@
 
     def inject(t):
         left = jnp.concatenate(parts(one(high == high32) * arrive[t]), axis=0)
-        jl[t] = third_sum(nt(left, ohl[...])).reshape(DEVS, 8, 128)
+        jl[t] = add_parts(nt(left, ohl[...])).reshape(DEVS, 8, 128)
 
     def sample(v):
         left = jnp.concatenate(parts(v), axis=0)
-        return rows_sum(third_sum(nn(left, ohl[...])) * one(high == row_high))
+        return rows_sum(add_parts(nn(left, ohl[...])) * one(high == row_high))
 
     arrive = [arrivals(0), arrivals(1)]
     inject(0)
@@ -366,48 +391,66 @@
         for k in FAR_FIRST:
             r_copy(b, k).start()
 
-    def at_models(b):
-        r_all(b).wait_recv()
-        return parts(rrecv[b, :, 0, :])
-
-    product(3)
-    product(4)
+    def last_copy(g):
+        return copy(lsend.at[g // NETS, g % NETS // 8], lrecv.at[g], e_s, e_r, away(g % NETS, -1), dev(g // NETS))
+
+    def last_all():
+        rest = pl.ds(1, NETS * DEVS - 1)
+        return copy(lrecv.at[rest], lrecv.at[rest], e_s, e_r, away(1), d)
+
+    def send_last(early, late):
+        left = jnp.concatenate(parts(jnp.concatenate([early, late], axis=0)), axis=0)
+        for j in range(DEVS):
+            found = add_parts(nn(left, hots[j]))
+            for i in range(2):
+                line = rows_sum(found[8 * i:8 * i + 8] * brow[j])
+                for g in range(4):
+                    lsend[j, g, i:i + 1, :] = line[:, 128 * g:128 * g + 128]
+        lrecv[0] = lsend[0, 0]
+        for g in ALL_FAR_FIRST:
+            last_copy(g).start()
+
     free, gain, volts = [], [], []
-    got = place_batch(0)
-    free += got[:2]
-    gain += got[2:]
+    passes(2, b=1, r=1)
+    first_all().wait_recv()
+    got = place_batch(0, 7)
+    free += got[:4]
+    gain += got[4:]
     for load in loads[11:]:
         load.wait()
     for c in range(DEVS):
         uv[0, c, 0] = jnp.concatenate([src[s, c] for s in range(4)], axis=0) + free[0][8 * c:8 * c + 8]
     base = jnp.concatenate([src[s, d] for s in range(4)], axis=0)
     for t in range(STEPS):
-        if t == 1:
-            share_batch(1)
         if 1 <= t <= STEPS - DMIN:
             send_waves(t - 1)
         if t == 1:
-            send_batch(2, free_m[4:6] + gain_m[3:5])
+            send_batch(1, [free_of(2, 2), gain_of(1, 2), gain_of(2, 2)])
+            passes(3, x=2, b=2, r=2)
         if t == 2:
-            product(5)
-        if t == 3:
-            product(6)
-            send_batch(3, free_m[6:8] + gain_m[5:7])
-        if t == 4:
-            product(7)
+            passes(4, x=3)
+            send_batch(2, [free_of(3, 2), free_of(3, 3), free_of(4, 3), gain_of(3, 2), gain_of(3, 3)])
         if t >= 2:
             take_waves(t - 2)
         if t == 2:
+            share_batch(1)
+        if t == 3:
+            got = place_batch(1, 3)
+            free += got[:1]
+            gain += got[1:]
+            passes(5, x=4)
             share_batch(2)
         if t == 4:
-            share_batch(3)
-        if t % 2:
-            got = place_batch((t + 1) // 2) if t < 7 else []
-            free += got[:2]
-            gain += got[2:]
-        if t >= 5:
-            for old in ((0, 1), (2, 3), (4, 5))[t - 5]:
-                keep(old)
+            passes(6, x=5)
+            got = place_batch(2, 5)
+            free += got[:3]
+            gain += got[3:]
+        if t == 5:
+            passes(7, x=6, b=3)
+        if t == 6:
+            passes(8, x=7, b=4)
+        if t == 7:
+            send_back(0, list(range(STEPS - 2)))
         ready = base
         if t + 1 < STEPS:
             ready = ready + free[t + 1]
@@ -416,15 +459,15 @@
         v = solve(t)
         volts.append(v)
         uv_send(t + 1, ready + gain[0] * v if t + 1 < STEPS else jnp.zeros((8, 128), F32), v)
-    send_back(0, list(range(STEPS - 1)))
-    for j in range(1, DEVS):
-        uv_wait(STEPS, j).wait_recv()
-    send_back(1, [STEPS - 1])
-
-    keep(STEPS - 2)
-    keep(STEPS - 1)
+    send_last(volts[-2], volts[-1])
+
+    passes(9, b=5)
+    passes(10, b=6)
+    for t in range(STEPS - 1):
+        keep(t)
     line_copy.wait_send()
-    for b in range(4):
+    first_all().wait_send()
+    for b in range(1, 3):
         a_all(b).wait_send()
         for j in range(1, DEVS):
             v_copy(b, j).wait_send()
@@ -432,16 +475,27 @@
         uv_all(t).wait_send()
     for t in range(STEPS - DMIN):
         w_all(t).wait_send()
-    state = xs[...]
-    by_seat = sum(tn(piece, own) for piece in at_models(0))
-    for t in range(STEPS - 1):
+    r_all(0).wait_recv()
+    by_seat = sum(tn(piece, own) for piece in parts(rrecv[0, :, 0, :]))
+    state = xp[8]
+    for t in range(STEPS - 2):
         state = state + rows_sum(by_seat[CAP * t:CAP * t + CAP] * seat) * xb[STEPS - 1 - t]
     state = state.T
-    seat_cols = jnp.concatenate([seat, jnp.zeros((128 - CAP, 128), F32)], axis=0).T
-    for b in range(2):
-        r_all(b).wait_send()
-    by_model = sum(tn(own, piece) for piece in at_models(1))
-    final[...] = state + jnp.sum(by_model * seat_cols, axis=1, keepdims=True) * gi[...]
+    next_gain = xb[1].T
+    spot = CAP * (offset - 8.0 * jnp.floor(offset * 0.125)) + rank
+    spots = one(iota_f((128, 128), 0) == spot).T
+    r_all(0).wait_send()
+    for j in range(1, DEVS):
+        uv_wait(STEPS, j).wait_recv()
+    keep(STEPS - 1)
+    last_all().wait_recv()
+    columns_of = []
+    for i in range(2):
+        answer = sum(lrecv[NETS * j:NETS * j + NETS, i, :] for j in range(DEVS))
+        by_model = sum(tn(own, piece) for piece in parts(answer))
+        columns_of.append(jnp.sum(by_model * spots, axis=1, keepdims=True))
+    final[...] = state + columns_of[0] * next_gain + columns_of[1] * gi[...]
+    last_all().wait_send()
 
 
 def body(zinv, source, model_state, propagator, input_gain, output_gain, model_owner, model_bus,
@@ -452,15 +506,16 @@
         vmem((4, 256, 1024), F32), vmem((4, DEVS, 2, 128), F32), vmem((128, 128), F32), vmem((128, 128), F32),
         vmem((128, 128), F32), vmem((1, 128), i32), vmem((1, 128), i32), vmem((1, 512), i32), vmem((1, 512), i32),
         vmem((1, 512), i32), vmem((1, 512), F32), vmem((DMAX, 512), F32), vmem((DMAX, 512), F32),
-        vmem((16, 128, 8, 128), F32), vmem((128, 128, 128), F32), vmem((128, 128), F32), vmem((128, 128), F32),
-        vmem((STEPS, 128, 128), F32), vmem((4, NETS, 1, 128), F32), vmem((4, NETS, 1, 128), F32),
-        vmem((4, DEVS, 8, 512), F32), vmem((STEPS + 1, DEVS, 2, 8, 128), F32), vmem((16, 512), F32),
+        vmem((16, 128, 8, 128), F32), vmem((128, 128, 128), F32), vmem((STEPS + 1, 128, 128), F32),
+        vmem((STEPS, 128, 128), F32), vmem((4, 128, 128), F32), vmem((3, NETS, 1, 128), F32),
+        vmem((3, NETS, 1, 128), F32), vmem((NETS * DEVS, 1, 128), F32), vmem((3, DEVS, 8, 512), F32), vmem((STEPS + 1, DEVS, 2, 8, 128), F32), vmem((16, 512), F32),
         vmem((16, 512), F32), vmem((6, 2, 1, 512), F32), vmem((6, 2, DEVS, 1, 512), F32),
-        vmem((2, NETS, 1, 128), F32), vmem((2, NETS, 1, 128), F32), vmem((128, 1024), BF16),
+        vmem((1, NETS, 1, 128), F32), vmem((1, NETS, 1, 128), F32),
+        vmem((DEVS, 4, 2, 128), F32), vmem((NETS * DEVS, 2, 128), F32), vmem((128, 1024), BF16),
         vmem((DEVS, 128, 512), BF16), vmem((DEVS, 8, 512), F32), vmem((4, 256, 128), F32),
         vmem((STEPS, DEVS, 8, 128), F32),
-        dma((13,)), dma((16,)), dma((4,)), dma((4,)), dma((4, DEVS)), dma((4, DEVS)),
-        dma((STEPS + 1,)), dma((STEPS + 1, DEVS)), dma((6,)), dma((6,)), dma, dma, dma((2,)), dma((2,)),
+        dma((13,)), dma((16,)), dma((3,)), dma((3,)), dma((3, DEVS)), dma((3, DEVS)),
+        dma((STEPS + 1,)), dma((STEPS + 1, DEVS)), dma((6,)), dma((6,)), dma, dma, dma((1,)), dma((1,)), dma, dma,
     ]
     v = pl.BlockSpec(memory_space=vmem)
     return pl.pallas_call(

time: 62.1 us -> 57.2 us (0.921)
  Pallas kernels: 60.1 us -> 55.1 us
    pallas_call x1, Pallas kernels: 60.1 us -> 55.1 us  [body(): pl.pallas_call(grid_kernel, out_shape=(vmem((STEPS, 4096), F32), vmem((12...]
where the time goes in v4:
time: 57.2 us; the launch traced here: 57.1 us
  Pallas kernels  55.1 us (96%)
  local copies, waits for them, and re-layouts  1.29 us (2%)
  between operations  0.64 us (1%)
    pallas_call x1, Pallas kernels, body(): pl.pallas_call(grid_kernel, out_shape=(vmem((STEPS, 4096), F32), vmem((12...  55.1 us
    unnamed x2, local copies, waits for them, and re-layouts  1.29 us

profile of v4, /device:TPU:1, one launch (start us, length us, event | category | flops | bytes accessed | tf_op | source)
XLA Modules:
  0.0 57.1 jit_solution(733022657218770241)
XLA Ops:
  0.6 55.1 %shard_map.149 = (f32[8,4096]{1,0:T(8,128)S(1)}, f32[128,128]{1,0:T(8,128)S(1)}) custom-call(f32[4,256,1024]{2,1,0:T(8,128)} %zinv.1, f32[4,4,2,128]{3,2,1,0:T(2,128)} %bitcast.7, f32[128,128]{1,0:T(8,128)} %state0.1, f32[128,128,128]{2,1,0:T(8,128)} %prop.1, f32[128,128]{1,0:T(8,128)} %bgain.1, f32[128,128]{1,0:T(8,128)} %ogain.1, s32[1,128]{1,0:T(1,128)} %bitcast.12, ...), custom_call_target="tpu_custom_call" | custom-call | tf_op jit(solution)/shard_map/pallas_call | solution.py:521
  55.8 0.7 %copy.18 = f32[8,4096]{1,0:T(8,128)} copy(f32[8,4096]{1,0:T(8,128)S(1)} %get-tuple-element.2) | data formatting | bytes 262144
  56.4 0.6 %copy.19 = f32[128,128]{1,0:T(8,128)} copy(f32[128,128]{1,0:T(8,128)S(1)} %get-tuple-element.3) | data formatting | bytes 131072

commit v5 on v4

--- a/solution.py
+++ b/solution.py
@@ -76,9 +76,9 @@
 def grid_kernel(zinv, source, state0, prop, bgain, ogain, owner_i, bus_i, from_i, to_i, delay_i, imped_i, fpast, tpast,
                 trace, final,
                 z, src, st, gi, go, own_v, bus_v, from_v, to_v, delay_v, imped_v, fp, tp,
-                raw, at, xp, xb, rp, asend, arecv, arecv0, vall, uv, pack, prev, wsend, wrecv, rsend, rrecv, lsend, lrecv,
+                raw, at, xp, xb, rp, asend, arecv, arecv0, vall, um, vv, pack, prev, wsend, wrecv, rsend, rrecv, lsend, lrecv,
                 ohl, hots, brow, acc, jl,
-                in_s, raw_s, a_s, a_r, v_s, v_r, uv_s, uv_r, w_s, w_r, l_s, l_r, r_s, r_r, e_s, e_r):
+                in_s, raw_s, a_s, a_r, v_s, v_r, um_s, um_r, vv_s, vv_r, w_s, w_r, l_s, l_r, r_s, r_r, e_s, e_r):
     n = lax.axis_index("net")
     d = lax.axis_index("dev")
 
@@ -87,14 +87,13 @@
     core = n % 2
 
     def net(k):
-        return lax.rem(n + k, NETS)
+        return (n + k) & (NETS - 1)
 
     def away(k, way=1):
-        kx, ky, kc = way * (k // 8) + 4, way * ((k // 2) % 4) + 4, k % 2
-        return lax.rem(x + kx, 4) * 8 + lax.rem(y + ky, 4) * 2 + lax.rem(core + kc, 2)
+        return (((x + way * (k // 8)) & 3) * 8) + (((y + way * (k // 2 % 4)) & 3) * 2) + ((core + k) & 1)
 
     def dev(j):
-        return lax.rem(d + j, DEVS)
+        return (d + j) & (DEVS - 1)
 
     def copy(a, b, send, recv, to_net, to_dev):
         return pltpu.make_async_remote_copy(src_ref=a, dst_ref=b, send_sem=send, recv_sem=recv,
@@ -107,11 +106,11 @@
     def raw_copy(c):
         return pltpu.make_async_copy(prop.at[:, pl.ds(8 * c, 8), :], raw.at[c], raw_s.at[c])
 
-    for load in loads[:11]:
+    for load in loads[:3]:
         load.start()
     for c in range(16):
         raw_copy(c).start()
-    for load in loads[11:]:
+    for load in loads[3:]:
         load.start()
 
     bar = pltpu.get_barrier_semaphore()
@@ -119,41 +118,14 @@
     def greet(to_net, to_dev):
         pl.semaphore_signal(bar, inc=1, device_id=(to_net, to_dev), device_id_type=MESH)
 
-    def greet_all(k, _):
-        for j in range(DEVS):
-            greet(net(k), dev(j))
-        return 0
-
-    lax.fori_loop(1, NETS, greet_all, 0)
-    for j in range(1, DEVS):
-        greet(n, dev(j))
-
-    for load in loads[:11]:
+    for g in ALL_FAR_FIRST:
+        greet(away(g % NETS), dev(g // NETS))
+
+    for load in loads[:3]:
         load.wait()
-    owner = own_v[...].astype(F32)
-    own_x = jnp.floor(owner * 0.125)
-    own_y = jnp.floor((owner - 8.0 * own_x) * 0.5)
-    own_c = owner - 8.0 * own_x - 2.0 * own_y
-
-    def steps_to(to, at, size):
-        gap = to - at.astype(F32)
-        return jnp.where(gap < 0.0, gap + size, gap)
-
-    offset = 8.0 * steps_to(own_x, x, 4.0) + 2.0 * steps_to(own_y, y, 4.0) + steps_to(own_c, core, 2.0)
-    wide = jnp.broadcast_to(owner, (128, 128))
-    earlier = one(wide.T == wide) * one(iota((128, 128), 0) < iota((128, 128), 1))
-    rank = rows_sum(earlier)
-    own = one(iota_f((NETS, 128), 0) == offset).astype(BF16)
-    seat = one(iota_f((CAP, 128), 0) == rank)
     xp[0] = st[...].T
     xb[0] = gi[...].T
     rp[0] = go[...].T
-    pack[0:1, :] = to_v[...].astype(F32)
-    pack[1:2, :] = delay_v[...].astype(F32)
-    pack[2:3, :] = imped_v[...]
-    pack[3:9, :] = fp[...]
-    pack[9:16, :] = jnp.zeros((7, 512), F32)
-
     flat = raw.reshape(16, 1024, 128)
     zero = jnp.zeros((128, 128), F32)
 
@@ -186,6 +158,31 @@
         if b is not None:
             xb[b + 1] = ab
 
+    passes(0, x=0, b=0, r=0)
+
+    for load in loads[3:11]:
+        load.wait()
+    owner = own_v[...].astype(F32)
+    own_x = jnp.floor(owner * 0.125)
+    own_y = jnp.floor((owner - 8.0 * own_x) * 0.5)
+    own_c = owner - 8.0 * own_x - 2.0 * own_y
+
+    def steps_to(to, at, size):
+        gap = to - at.astype(F32)
+        return jnp.where(gap < 0.0, gap + size, gap)
+
+    offset = 8.0 * steps_to(own_x, x, 4.0) + 2.0 * steps_to(own_y, y, 4.0) + steps_to(own_c, core, 2.0)
+    wide = jnp.broadcast_to(owner, (128, 128))
+    earlier = one(wide.T == wide) * one(iota((128, 128), 0) < iota((128, 128), 1))
+    rank = rows_sum(earlier)
+    own = one(iota_f((NETS, 128), 0) == offset).astype(BF16)
+    seat = one(iota_f((CAP, 128), 0) == rank)
+    pack[0:1, :] = to_v[...].astype(F32)
+    pack[1:2, :] = delay_v[...].astype(F32)
+    pack[2:3, :] = imped_v[...]
+    pack[3:9, :] = fp[...]
+    pack[9:16, :] = jnp.zeros((7, 512), F32)
+
     def free_of(i, j):
         return rows_sum(xp[i] * rp[j])
 
@@ -267,7 +264,6 @@
         total = add_parts(total)
         return [total[:first_rows]] + [total[first_rows + 8 * q:first_rows + 8 * q + 8] for q in range(count - 1)]
 
-    passes(0, x=0, b=0, r=0)
     passes(1, x=1)
     pl.semaphore_wait(bar, NETS * DEVS - 1)
     line_copy = copy(pack, prev, l_s, l_r, net(1), d)
@@ -303,21 +299,19 @@
     inject(0)
     inject(1)
 
-    def uv_copy(t, j):
-        return copy(uv.at[t, d], uv.at[t, d], uv_s.at[t], uv_r.at[t, d], n, dev(j))
-
-    def uv_wait(t, j):
-        return copy(uv.at[t, dev(j)], uv.at[t, dev(j)], uv_s.at[t], uv_r.at[t, dev(j)], n, dev(j))
-
-    def uv_all(t):
-        sent = uv.at[t, pl.ds(0, DEVS - 1)]
-        return copy(sent, sent, uv_s.at[t], uv_r.at[t, d], n, dev(1))
-
-    def uv_send(t, u, v):
-        uv[t, d, 0] = u
-        uv[t, d, 1] = v
-        for j in (2, 1, 3):
-            uv_copy(t, j).start()
+    def um_copy(t, j):
+        return copy(um.at[t, d], um.at[t, d], um_s.at[t], um_r.at[t, d], n, dev(j))
+
+    def um_wait(t, j):
+        return copy(um.at[t, dev(j)], um.at[t, dev(j)], um_s.at[t], um_r.at[t, dev(j)], n, dev(j))
+
+    def um_all(t):
+        sent = um.at[t, pl.ds(0, DEVS - 1)]
+        return copy(sent, sent, um_s.at[t], um_r.at[t, d], n, dev(1))
+
+    def vv_copy(half, j, sender):
+        steps = pl.ds(0, STEPS - 2) if half == 0 else pl.ds(STEPS - 2, 2)
+        return copy(vv.at[sender, steps], vv.at[sender, steps], vv_s.at[half, j], vv_r.at[half, sender], n, dev(j))
 
     def w_copy(t, way, j):
         return copy(wsend.at[t, way], wrecv.at[t, way, d], w_s.at[t], w_r.at[t], net(1 if way == 0 else NETS - 1), dev(j))
@@ -341,7 +335,7 @@
         inject(t + DMIN)
 
     def columns(t, c, s):
-        tiles = uv[t, c, 0] + jl[t, c]
+        tiles = um[t, c] + jl[t, c]
         total = None
         for e in range(2):
             lanes = pl.ds(pl.multiple_of(256 * c + 128 * e, 128), 128)
@@ -350,13 +344,15 @@
         return total
 
     def solve(t):
+        for s in range(4):
+            acc[s] = columns(t, d, s)
         if t:
-            uv_wait(t, 1).wait_recv()
-            uv_wait(t, 3).wait_recv()
+            um_wait(t, 1).wait_recv()
+            um_wait(t, 3).wait_recv()
         for s in range(4):
-            acc[s] = columns(t, d, s) + columns(t, dev(1), s) + columns(t, dev(3), s)
+            acc[s] = acc[s] + columns(t, dev(1), s) + columns(t, dev(3), s)
         if t:
-            uv_wait(t, 2).wait_recv()
+            um_wait(t, 2).wait_recv()
         rows = []
         for s in range(4):
             total = acc[s] + columns(t, dev(2), s)
@@ -368,7 +364,7 @@
         for c in range(8):
             for s in range(4):
                 spot = 1024 * s + 128 * c
-                trace[t:t + 1, spot:spot + 128] = uv[t + 1, c // 2, 1, 2 * s + c % 2:2 * s + c % 2 + 1, :]
+                trace[t:t + 1, spot:spot + 128] = vv[c // 2, t, 2 * s + c % 2:2 * s + c % 2 + 1, :]
 
     def r_copy(b, k):
         return copy(rsend.at[b, k], rrecv.at[b, k], r_s.at[b], r_r.at[b], away(k, -1), d)
@@ -378,7 +374,7 @@
         return copy(rsend.at[b, rest], rrecv.at[b, rest], r_s.at[b], r_r.at[b], away(1), d)
 
     def send_back(b, steps):
-        full = jnp.concatenate([uv[t + 1, c, 1] for t in steps for c in range(DEVS)], axis=0)
+        full = jnp.concatenate([vv[c, t] for t in steps for c in range(DEVS)], axis=0)
         reached = sum(nn(piece, hots[0]) for piece in parts(full))
         pick = one(slot_high[0] == high32)
         seats = one(iota((CAP, 512), 1) % CAP == iota((CAP, 512), 0))
@@ -419,7 +415,7 @@
     for load in loads[11:]:
         load.wait()
     for c in range(DEVS):
-        uv[0, c, 0] = jnp.concatenate([src[s, c] for s in range(4)], axis=0) + free[0][8 * c:8 * c + 8]
+        um[0, c] = jnp.concatenate([src[s, c] for s in range(4)], axis=0) + free[0][8 * c:8 * c + 8]
     base = jnp.concatenate([src[s, d] for s in range(4)], axis=0)
     for t in range(STEPS):
         if 1 <= t <= STEPS - DMIN:
@@ -448,8 +444,12 @@
         if t == 5:
             passes(7, x=6, b=3)
         if t == 6:
+            for j in (2, 1, 3):
+                vv_copy(0, j, d).start()
             passes(8, x=7, b=4)
         if t == 7:
+            for j in range(1, DEVS):
+                vv_copy(0, j, dev(j)).wait_recv()
             send_back(0, list(range(STEPS - 2)))
         ready = base
         if t + 1 < STEPS:
@@ -458,12 +458,18 @@
                 ready = ready + gain[t - k] * volts[k]
         v = solve(t)
         volts.append(v)
-        uv_send(t + 1, ready + gain[0] * v if t + 1 < STEPS else jnp.zeros((8, 128), F32), v)
+        if t + 1 < STEPS:
+            um[t + 1, d] = ready + gain[0] * v
+            for j in (2, 1, 3):
+                um_copy(t + 1, j).start()
+        vv[d, t] = v
+    for j in (2, 1, 3):
+        vv_copy(1, j, d).start()
     send_last(volts[-2], volts[-1])
 
     passes(9, b=5)
     passes(10, b=6)
-    for t in range(STEPS - 1):
+    for t in range(STEPS - 2):
         keep(t)
     line_copy.wait_send()
     first_all().wait_send()
@@ -471,8 +477,11 @@
         a_all(b).wait_send()
         for j in range(1, DEVS):
             v_copy(b, j).wait_send()
-    for t in range(1, STEPS + 1):
-        uv_all(t).wait_send()
+    for t in range(1, STEPS):
+        um_all(t).wait_send()
+    for j in range(1, DEVS):
+        vv_copy(0, j, d).wait_send()
+        vv_copy(1, j, d).wait_send()
     for t in range(STEPS - DMIN):
         w_all(t).wait_send()
     r_all(0).wait_recv()
@@ -486,7 +495,8 @@
     spots = one(iota_f((128, 128), 0) == spot).T
     r_all(0).wait_send()
     for j in range(1, DEVS):
-        uv_wait(STEPS, j).wait_recv()
+        vv_copy(1, j, dev(j)).wait_recv()
+    keep(STEPS - 2)
     keep(STEPS - 1)
     last_all().wait_recv()
     columns_of = []
@@ -508,14 +518,14 @@
         vmem((1, 512), i32), vmem((1, 512), F32), vmem((DMAX, 512), F32), vmem((DMAX, 512), F32),
         vmem((16, 128, 8, 128), F32), vmem((128, 128, 128), F32), vmem((STEPS + 1, 128, 128), F32),
         vmem((STEPS, 128, 128), F32), vmem((4, 128, 128), F32), vmem((3, NETS, 1, 128), F32),
-        vmem((3, NETS, 1, 128), F32), vmem((NETS * DEVS, 1, 128), F32), vmem((3, DEVS, 8, 512), F32), vmem((STEPS + 1, DEVS, 2, 8, 128), F32), vmem((16, 512), F32),
+        vmem((3, NETS, 1, 128), F32), vmem((NETS * DEVS, 1, 128), F32), vmem((3, DEVS, 8, 512), F32), vmem((STEPS, DEVS, 8, 128), F32), vmem((DEVS, STEPS, 8, 128), F32), vmem((16, 512), F32),
         vmem((16, 512), F32), vmem((6, 2, 1, 512), F32), vmem((6, 2, DEVS, 1, 512), F32),
         vmem((1, NETS, 1, 128), F32), vmem((1, NETS, 1, 128), F32),
         vmem((DEVS, 4, 2, 128), F32), vmem((NETS * DEVS, 2, 128), F32), vmem((128, 1024), BF16),
         vmem((DEVS, 128, 512), BF16), vmem((DEVS, 8, 512), F32), vmem((4, 256, 128), F32),
         vmem((STEPS, DEVS, 8, 128), F32),
         dma((13,)), dma((16,)), dma((3,)), dma((3,)), dma((3, DEVS)), dma((3, DEVS)),
-        dma((STEPS + 1,)), dma((STEPS + 1, DEVS)), dma((6,)), dma((6,)), dma, dma, dma((1,)), dma((1,)), dma, dma,
+        dma((STEPS,)), dma((STEPS, DEVS)), dma((2, DEVS)), dma((2, DEVS)), dma((6,)), dma((6,)), dma, dma, dma((1,)), dma((1,)), dma, dma,
     ]
     v = pl.BlockSpec(memory_space=vmem)
     return pl.pallas_call(

time: 57.2 us -> 55.6 us (0.972)
  Pallas kernels: 55.1 us -> 53.6 us
    pallas_call x1, Pallas kernels: 55.1 us -> 53.6 us  [body(): pl.pallas_call(grid_kernel, out_shape=(vmem((STEPS, 4096), F32), vmem((12...]
where the time goes in v5:
time: 55.6 us; the launch traced here: 55.5 us
  Pallas kernels  53.6 us (96%)
  local copies, waits for them, and re-layouts  1.29 us (2%)
  between operations  0.64 us (1%)
    pallas_call x1, Pallas kernels, body(): pl.pallas_call(grid_kernel, out_shape=(vmem((STEPS, 4096), F32), vmem((12...  53.6 us
    unnamed x2, local copies, waits for them, and re-layouts  1.29 us

profile of v5, /device:TPU:1, one launch (start us, length us, event | category | flops | bytes accessed | tf_op | source)
XLA Modules:
  0.0 55.5 jit_solution(14600637406847667231)
XLA Ops:
  0.6 53.6 %shard_map.149 = (f32[8,4096]{1,0:T(8,128)S(1)}, f32[128,128]{1,0:T(8,128)S(1)}) custom-call(f32[4,256,1024]{2,1,0:T(8,128)} %zinv.1, f32[4,4,2,128]{3,2,1,0:T(2,128)} %bitcast.7, f32[128,128]{1,0:T(8,128)} %state0.1, f32[128,128,128]{2,1,0:T(8,128)} %prop.1, f32[128,128]{1,0:T(8,128)} %bgain.1, f32[128,128]{1,0:T(8,128)} %ogain.1, s32[1,128]{1,0:T(1,128)} %bitcast.12, ...), custom_call_target="tpu_custom_call" | custom-call | tf_op jit(solution)/shard_map/pallas_call | solution.py:531
  54.2 0.7 %copy.18 = f32[8,4096]{1,0:T(8,128)} copy(f32[8,4096]{1,0:T(8,128)S(1)} %get-tuple-element.2) | data formatting | bytes 262144
  54.9 0.6 %copy.19 = f32[128,128]{1,0:T(8,128)} copy(f32[128,128]{1,0:T(8,128)S(1)} %get-tuple-element.3) | data formatting | bytes 131072

commit v6 on v5

--- a/solution.py
+++ b/solution.py
@@ -508,6 +508,14 @@
     last_all().wait_send()
 
 
+def hand_out(trace, final, trace_out, final_out, sems):
+    copies = [pltpu.make_async_copy(trace, trace_out, sems.at[0]), pltpu.make_async_copy(final, final_out, sems.at[1])]
+    for one_copy in copies:
+        one_copy.start()
+    for one_copy in copies:
+        one_copy.wait()
+
+
 def body(zinv, source, model_state, propagator, input_gain, output_gain, model_owner, model_bus,
          line_from, line_to, line_delay, line_imped, wave_from_past, wave_to_past):
     vmem, dma = pltpu.VMEM, pltpu.SemaphoreType.DMA
@@ -528,7 +536,7 @@
         dma((STEPS,)), dma((STEPS, DEVS)), dma((2, DEVS)), dma((2, DEVS)), dma((6,)), dma((6,)), dma, dma, dma((1,)), dma((1,)), dma, dma,
     ]
     v = pl.BlockSpec(memory_space=vmem)
-    return pl.pallas_call(
+    found = pl.pallas_call(
         grid_kernel,
         out_shape=(vmem((STEPS, 4096), F32), vmem((128, 128), F32)),
         in_specs=[pl.BlockSpec(memory_space=pl.ANY)] * 14,
@@ -538,6 +546,14 @@
     )(zinv, source.reshape(4, DEVS, 2, 128), model_state, propagator, input_gain, output_gain,
       model_owner.reshape(1, 128), model_bus.reshape(1, 128), line_from.reshape(1, 512), line_to.reshape(1, 512),
       line_delay.reshape(1, 512), line_imped.reshape(1, 512), wave_from_past, wave_to_past)
+    return pl.pallas_call(
+        hand_out,
+        out_shape=(jax.ShapeDtypeStruct((STEPS, 4096), F32), jax.ShapeDtypeStruct((128, 128), F32)),
+        in_specs=[v, v],
+        out_specs=(pl.BlockSpec(memory_space=pl.ANY), pl.BlockSpec(memory_space=pl.ANY)),
+        scratch_shapes=[dma((2,))],
+        compiler_params=pltpu.CompilerParams(vmem_limit_bytes=40 << 20),
+    )(*found)
 
 
 def solution(mesh):

time: 55.6 us -> 55 us (0.989)
  local copies, waits for them, and re-layouts: 1.29 us -> 0 us
  Pallas kernels: 53.6 us -> 54.2 us
    unnamed x2 -> x0, local copies, waits for them, and re-layouts: 1.29 us -> none
    pallas_call x0 -> x1, Pallas kernels: none -> 0.69 us  [body(): pl.pallas_call(hand_out, out_shape=(jax.ShapeDtypeStruct((STEPS, 4096), F...]
where the time goes in v6:
time: 55 us; the launch traced here: 54.9 us
  Pallas kernels  54.2 us (99%)
  between operations  0.64 us (1%)
    pallas_call x1, Pallas kernels, body(): pl.pallas_call(grid_kernel, out_shape=(vmem((STEPS, 4096), F32), vmem((12...  53.6 us

profile of v6, /device:TPU:1, one launch (start us, length us, event | category | flops | bytes accessed | tf_op | source)
XLA Modules:
  0.0 54.9 jit_solution(8421866847202001525)
XLA Ops:
  0.6 53.6 %shard_map.149 = (f32[8,4096]{1,0:T(8,128)S(1)}, f32[128,128]{1,0:T(8,128)S(1)}) custom-call(f32[4,256,1024]{2,1,0:T(8,128)} %zinv.1, f32[4,4,2,128]{3,2,1,0:T(2,128)} %bitcast.7, f32[128,128]{1,0:T(8,128)} %state0.1, f32[128,128,128]{2,1,0:T(8,128)} %prop.1, f32[128,128]{1,0:T(8,128)} %bgain.1, f32[128,128]{1,0:T(8,128)} %ogain.1, s32[1,128]{1,0:T(1,128)} %bitcast.12, ...), custom_call_target="tpu_custom_call" | custom-call | tf_op jit(solution)/shard_map/pallas_call | solution.py:539
  54.2 0.7 %shard_map.150 = (f32[8,4096]{1,0:T(8,128)}, f32[128,128]{1,0:T(8,128)}) custom-call(f32[8,4096]{1,0:T(8,128)S(1)} %get-tuple-element.4.trace, f32[128,128]{1,0:T(8,128)S(1)} %get-tuple-element.5.final), custom_call_target="tpu_custom_call" | custom-call | tf_op jit(solution)/shard_map/pallas_call | solution.py:549

commit v7 on v6

--- a/solution.py
+++ b/solution.py
@@ -394,16 +394,20 @@
         rest = pl.ds(1, NETS * DEVS - 1)
         return copy(lrecv.at[rest], lrecv.at[rest], e_s, e_r, away(1), d)
 
-    def send_last(early, late):
-        left = jnp.concatenate(parts(jnp.concatenate([early, late], axis=0)), axis=0)
+    def pick_last(i, v):
+        left = jnp.concatenate(parts(v), axis=0)
         for j in range(DEVS):
-            found = add_parts(nn(left, hots[j]))
-            for i in range(2):
-                line = rows_sum(found[8 * i:8 * i + 8] * brow[j])
-                for g in range(4):
-                    lsend[j, g, i:i + 1, :] = line[:, 128 * g:128 * g + 128]
+            line = rows_sum(add_parts(nn(left, hots[j])) * brow[j])
+            for g in range(4):
+                lsend[j, g, i:i + 1, :] = line[:, 128 * g:128 * g + 128]
+
+    def send_last():
         lrecv[0] = lsend[0, 0]
-        for g in ALL_FAR_FIRST:
+        for g in ALL_FAR_FIRST[:30]:
+            last_copy(g).start()
+        for j in (2, 1, 3):
+            vv_copy(1, j, d).start()
+        for g in ALL_FAR_FIRST[30:]:
             last_copy(g).start()
 
     free, gain, volts = [], [], []
@@ -423,8 +427,8 @@
         if t == 1:
             send_batch(1, [free_of(2, 2), gain_of(1, 2), gain_of(2, 2)])
             passes(3, x=2, b=2, r=2)
+            passes(4, x=3)
         if t == 2:
-            passes(4, x=3)
             send_batch(2, [free_of(3, 2), free_of(3, 3), free_of(4, 3), gain_of(3, 2), gain_of(3, 3)])
         if t >= 2:
             take_waves(t - 2)
@@ -451,6 +455,7 @@
             for j in range(1, DEVS):
                 vv_copy(0, j, dev(j)).wait_recv()
             send_back(0, list(range(STEPS - 2)))
+            pick_last(0, volts[-1])
         ready = base
         if t + 1 < STEPS:
             ready = ready + free[t + 1]
@@ -463,9 +468,8 @@
             for j in (2, 1, 3):
                 um_copy(t + 1, j).start()
         vv[d, t] = v
-    for j in (2, 1, 3):
-        vv_copy(1, j, d).start()
-    send_last(volts[-2], volts[-1])
+    pick_last(1, volts[-1])
+    send_last()
 
     passes(9, b=5)
     passes(10, b=6)

time: 55 us -> 55.2 us (level)
  no operation moved by 1% of the time
where the time goes in v7:
time: 55.2 us; the launch traced here: 55.1 us
  Pallas kernels  54.5 us (99%)
  between operations  0.64 us (1%)
    pallas_call x1, Pallas kernels, body(): pl.pallas_call(grid_kernel, out_shape=(vmem((STEPS, 4096), F32), vmem((12...  53.8 us

profile of v7, /device:TPU:1, one launch (start us, length us, event | category | flops | bytes accessed | tf_op | source)
XLA Modules:
  0.0 55.1 jit_solution(14803180038741000790)
XLA Ops:
  0.6 53.8 %shard_map.149 = (f32[8,4096]{1,0:T(8,128)S(1)}, f32[128,128]{1,0:T(8,128)S(1)}) custom-call(f32[4,256,1024]{2,1,0:T(8,128)} %zinv.1, f32[4,4,2,128]{3,2,1,0:T(2,128)} %bitcast.7, f32[128,128]{1,0:T(8,128)} %state0.1, f32[128,128,128]{2,1,0:T(8,128)} %prop.1, f32[128,128]{1,0:T(8,128)} %bgain.1, f32[128,128]{1,0:T(8,128)} %ogain.1, s32[1,128]{1,0:T(1,128)} %bitcast.12, ...), custom_call_target="tpu_custom_call" | custom-call | tf_op jit(solution)/shard_map/pallas_call | solution.py:543
  54.4 0.7 %shard_map.150 = (f32[8,4096]{1,0:T(8,128)}, f32[128,128]{1,0:T(8,128)}) custom-call(f32[8,4096]{1,0:T(8,128)S(1)} %get-tuple-element.4.trace, f32[128,128]{1,0:T(8,128)S(1)} %get-tuple-element.5.final), custom_call_target="tpu_custom_call" | custom-call | tf_op jit(solution)/shard_map/pallas_call | solution.py:553
